TPU v7x, 256 devices: a whole 4x4x8 slice. The times are simulated.
256 devices in a mesh: lat: 32 (over z, x), lyr: 4 (over y_lo, core), dp: 2 (over y_hi).
Axes of the slice: x: 4, y: 4 (y_hi: 2, y_lo: 2; y = y_hi * 2 + y_lo), z: 8, core: 2. Of those that a mesh axis runs over, the one named last changes fastest.
Arguments:
- act_codes: bfloat16 [1024, 4, 4096], P('dp', 'lyr'), may hold values from -6 to 6
- act_scales: bfloat16 [1024, 4, 32], P('dp', 'lyr'), may hold values from 0.25 to 2.5
- latents: bfloat16 [1024, 16384], P('dp', 'lat'), may hold values from 0 to 36, as said below
- dec_weight: bfloat16 [16384, 4, 4096], P('lat', 'lyr', 'dp'), may hold values from -0.296875 to 0.296875
- dec_bias: float32 [4, 4096], P('lyr'), may hold values from -3 to 3
Outputs:
- grad_enc: float32 [4096, 4, 16384], P('dp', 'lyr', 'lat')
- grad_dec: float32 [16384, 4, 4096], P('lat', 'lyr', 'dp')
- grad_bias: float32 [16384], P('lat')
Inputs may be any that keep to these rules, and one draw needn't show every extreme that they name: `latents`: nonnegative, with many exact zeros.
All inputs are finite; a program needn't handle non-finite values.
Results may differ from a plain program's by a relative error of at most 0.00065.
The roundings to bfloat16 on the way count: a program that leaves them out, or rounds other values in their place, can miss the bound.
Values may be sent and summed in bfloat16 or wider, within the bound.
A program may use at most 192 MiB of HBM per device.

v0:
```python
import jax
import jax.numpy as jnp
from jax import lax
from jax.sharding import PartitionSpec as P

penalty = 1.0
epsilon = 1e-06


def dequantize(code_block, scale_block):
    row_count, layer_count, width = code_block.shape
    block_count = scale_block.shape[2]
    scaled = (
        code_block.astype(jnp.float32).reshape(
            row_count, layer_count, block_count, width // block_count
        )
        * scale_block.astype(jnp.float32)[..., None]
    )
    return scaled.reshape(row_count, layer_count, width)


def reconstruct(act_rows, weight, inputs, bias_part):
    partial_value = jnp.einsum("rf,fld->rld", act_rows, weight, preferred_element_type=jnp.float32)
    recon = lax.psum(partial_value, "lat")
    return (recon + bias_part[None] - inputs).astype(jnp.bfloat16)


def shards(act_codes, act_scales, latents, dec_weight, dec_bias):
    local_squares = jnp.sum(jnp.square(dec_weight.astype(jnp.float32)), axis=2)
    inputs = dequantize(act_codes, act_scales)
    squares, act_sum = lax.psum((local_squares, jnp.sum(latents.astype(jnp.float32), axis=0)), "dp")
    weight = lax.all_gather(dec_weight, "dp", axis=2, tiled=True)
    inputs_bf = inputs.astype(jnp.bfloat16)
    row_norms = jnp.sqrt(squares + epsilon)
    norm_total = lax.psum(jnp.sum(row_norms, axis=1), "lyr")
    resid = reconstruct(latents, weight, inputs, dec_bias)
    grad_part = jnp.einsum("rld,fld->rf", resid, weight, preferred_element_type=jnp.float32)
    grad_sum = lax.psum(grad_part, "lyr")
    grad_pre = jnp.where(latents > 0, grad_sum + penalty * norm_total[None, :], 0.0).astype(
        jnp.bfloat16
    )
    scaled_rows = (penalty * act_sum[:, None] / row_norms)[:, :, None] * dec_weight.astype(
        jnp.float32
    )
    grad_bias = lax.psum(jnp.sum(grad_pre.astype(jnp.float32), axis=0), "dp")
    grad_enc = lax.psum_scatter(
        jnp.einsum("rld,rf->dlf", inputs_bf, grad_pre, preferred_element_type=jnp.float32),
        "dp",
        scatter_dimension=0,
        tiled=True,
    )
    dec_term = jnp.einsum("rf,rld->fld", latents, resid, preferred_element_type=jnp.float32)
    grad_dec = lax.psum_scatter(dec_term, "dp", scatter_dimension=2, tiled=True) + scaled_rows
    return (grad_enc, grad_dec, grad_bias)


def solution(mesh):
    in_specs = (
        P("dp", "lyr", None),
        P("dp", "lyr", None),
        P("dp", "lat"),
        P("lat", "lyr", "dp"),
        P("lyr", None),
    )
    out_specs = (P("dp", "lyr", "lat"), P("lat", "lyr", "dp"), P("lat"))
    return jax.shard_map(shards, mesh=mesh, in_specs=in_specs, out_specs=out_specs, check_vma=False)
```

profile of v0, /device:TPU:1, one launch (start us, length us, event | category | flops | bytes accessed | tf_op | source)
XLA Modules:
  0.0 594.7 jit_solution(6366850013612537920)
XLA Ops:
  7.2 0.0 all-gather.2.cloned.1.call-start
  7.2 0.7 all-gather.2.cloned.1.call-update
  7.9 0.0 all-reduce.4.cloned.1.call-start
  7.9 69.1 %all-gather.2.cloned.1.call-done = bf16[512,1,4096]{2,0,1:T(8,128)(2,1)} async-done(((bf16[512,1,2048]{2,0,1:T(8,128)(2,1)}), bf16[512,1,4096]{2,0,1:T(8,128)(2,1)}) %all-gather.2.cloned.1.call-update) | async-done | bytes 4194320 | tf_op jit(solution)/shard_map/all_gather | solution.py:32
  77.0 7.9 %convolution_bitcast_fusion.2 = f32[512,1,4096]{2,0,1:T(8,128)} fusion(bf16[512,512]{1,0:T(8,128)(2,1)} %param.7, bf16[512,1,4096]{2,0,1:T(8,128)(2,1)} %all-gather.2.cloned.1.call-done), kind=kOutput, calls=%fused_computation.4 | convolution fusion | flops 2147483648 | bytes 13107200 | tf_op jit(solution)/shard_map/rf,fld->rld/dot_general | solution.py:23
  84.9 0.0 all-reduce.4.cloned.1.call-update
  84.9 0.0 all-reduce.6.cloned.1.call-start
  85.0 0.7 copy-done.1
  85.7 0.1 copy.12
  85.8 5.7 mul.31
  91.5 9.5 %mul.32 = f32[512,1,4096]{2,0,1:T(8,128)} reshape(f32[512,32,128]{2,1,0:T(8,128)} %mul.31) | data formatting | bytes 16777216 | tf_op jit(solution)/shard_map/mul | solution.py:14
  101.0 195.2 %all-reduce.4.cloned.1.call-done = f32[512,1,4096]{2,0,1:T(8,128)} async-done(((f32[512,1,4096]{2,0,1:T(8,128)}), f32[512,1,4096]{2,0,1:T(8,128)}) %all-reduce.4.cloned.1.call-update) | async-done | bytes 8388624 | tf_op jit(solution)/shard_map/psum | solution.py:24
  296.1 11.7 %fusion.5 = bf16[512,4096]{1,0:T(8,128)(2,1)} fusion(f32[512,1,4096]{2,0,1:T(8,128)} %mul.32, bf16[512,1,4096]{2,0,1:T(8,128)(2,1)} %param.5, f32[512,1,4096]{2,0,1:T(8,128)} %all-reduce.4.cloned.1.call-done, f32[4096]{0:T(1024)S(1)} %bitcast.33), kind=kLoop, calls=%fused_computation.11 | loop fusion | flops 10485760 | bytes 25182208 | tf_op jit(solution)/shard_map/reshape.6
  307.8 6.8 %fusion.6 = f32[512,512]{1,0:T(8,128)} fusion(bf16[512,4096]{1,0:T(8,128)(2,1)} %fusion.5, bf16[512,1,4096]{2,0,1:T(8,128)(2,1)} %all-gather.2.cloned.1.call-done), kind=kOutput, calls=%fused_computation.12 | convolution fusion | flops 2147483648 | bytes 9437184 | tf_op jit(solution)/shard_map/rld,fld->rf/dot_general | solution.py:37
  314.7 0.0 reduce-scatter.5.cloned.1.call-start
  314.7 7.8 %convolution_bitcast_fusion = f32[512,1,4096]{0,2,1:T(8,128)} fusion(bf16[512,4096]{1,0:T(8,128)(2,1)} %fusion.5, bf16[512,512]{1,0:T(8,128)(2,1)S(1)} %copy-done), kind=kOutput, calls=%fused_computation.2 | convolution fusion | flops 2147483648 | bytes 13107200 | tf_op jit(solution)/shard_map/rf,rld->fld/dot_general | solution.py:52
  322.5 0.0 reduce-scatter.5.cloned.1.call-update
  322.5 0.0 reduce-scatter.3.cloned.1.call-start
  322.6 2.9 copy.13
  325.5 0.5 fusion.1
  326.0 5.3 psum.44
  331.3 7.0 %psum.45 = f32[512]{0:T(512)S(1)} all-reduce(f32[512]{0:T(512)S(1)} %bitcast.36), channel_id=1, replica_groups=mesh['lat'=32,'lyr'=4,'dp'=2] {'lyr'}, use_global_device_ids=true, to_apply=%region_4.0 | all-reduce | flops 512 | bytes 4096 | tf_op jit(solution)/shard_map/psum | solution.py:35
  338.4 22.0 %all-reduce.6.cloned.1.call-done = f32[512,512]{1,0:T(8,128)} async-done(((f32[512,512]{1,0:T(8,128)}), f32[512,512]{1,0:T(8,128)}) %all-reduce.6.cloned.1.call-update) | async-done | bytes 1048592 | tf_op jit(solution)/shard_map/psum | solution.py:38
  360.4 1.5 convert_reduce_fusion
  361.9 10.2 %convolution_bitcast_fusion.1 = f32[4096,1,512]{0,2,1:T(8,128)} fusion(bf16[512,512]{1,0:T(8,128)(2,1)S(1)} %get-tuple-element.12, f32[512,1,4096]{2,0,1:T(8,128)} %mul.32, bf16[512,1,4096]{2,0,1:T(8,128)(2,1)} %param.5), kind=kOutput, calls=%fused_computation.3 | convolution fusion | flops 2153775104 | bytes 21495808 | tf_op jit(solution)/shard_map/rld,rf->dlf/dot_general | solution.py:47
  372.1 0.0 reduce-scatter.3.cloned.1.call-update
  372.1 5.9 all-reduce
  378.0 91.6 %reduce-scatter.5.cloned.1.call-done = f32[512,1,2048]{0,2,1:T(8,128)} async-done(((f32[512,1,4096]{0,2,1:T(8,128)}), f32[512,1,2048]{0,2,1:T(8,128)}) %reduce-scatter.5.cloned.1.call-update) | async-done | bytes 4194320 | tf_op jit(solution)/shard_map/reduce_scatter | solution.py:53
  469.6 4.9 fusion.2
  474.5 11.0 %copy.15 = f32[512,1,2048]{2,1,0:T(1,128)} copy(f32[512,1,2048]{0,2,1:T(8,128)} %fusion.2) | data formatting | bytes 8388608
  485.4 91.9 %reduce-scatter.3.cloned.1.call-done = f32[2048,1,512]{0,2,1:T(8,128)} async-done(((f32[4096,1,512]{0,2,1:T(8,128)}), f32[2048,1,512]{0,2,1:T(8,128)}) %reduce-scatter.3.cloned.1.call-update) | async-done | bytes 4194320 | tf_op jit(solution)/shard_map/reduce_scatter | solution.py:46
  577.3 10.9 %copy.14 = f32[2048,1,512]{2,1,0:T(1,128)} copy(f32[2048,1,512]{0,2,1:T(8,128)} %reduce-scatter.3.cloned.1.call-done) | data formatting | bytes 8388608
  (9 shorter events, 0.1 us)
Async XLA Ops:
  7.2 69.8 %all-gather.2.cloned.1.call-start = ((), (), s32[]{:S(2)}) async-start(), calls=%async_computation.2 | async-start | bytes 6291456 | tf_op jit(solution)/shard_map/all_gather | solution.py:32
  7.9 288.2 %all-reduce.4.cloned.1.call-start = ((), (), s32[]{:S(2)}) async-start(), calls=%async_computation.3 | async-start | bytes 16777216 | tf_op jit(solution)/shard_map/psum | solution.py:24
  84.9 0.8 copy-start.1
  84.9 275.5 %all-reduce.6.cloned.1.call-start = ((), (), s32[]{:S(2)}) async-start(), calls=%async_computation.4 | async-start | bytes 2097152 | tf_op jit(solution)/shard_map/psum | solution.py:38
  91.5 204.6 %copy-start.2 = (f32[1,4096]{1,0:T(1,128)S(1)}, f32[1,4096]{1,0:T(1,128)}, u32[]{:S(2)}) copy-start(f32[1,4096]{1,0:T(1,128)} %param.9) | copy-start | bytes 49156
  307.8 6.9 %copy-start = (bf16[512,512]{1,0:T(8,128)(2,1)S(1)}, bf16[512,512]{1,0:T(8,128)(2,1)}, u32[]{:S(2)}) copy-start(bf16[512,512]{1,0:T(8,128)(2,1)} %param.7) | copy-start | bytes 1572868
  314.7 154.9 %reduce-scatter.5.cloned.1.call-start = ((), (), s32[]{:S(2)}) async-start(), calls=%async_computation.6 | async-start | bytes 12582912 | tf_op jit(solution)/shard_map/reduce_scatter | solution.py:53
  322.5 254.8 %reduce-scatter.3.cloned.1.call-start = ((), (), s32[]{:S(2)}) async-start(), calls=%async_computation.5 | async-start | bytes 12582912 | tf_op jit(solution)/shard_map/reduce_scatter | solution.py:46
Sparse Core Ops, SparseCore 0:
  9.8 67.1 all-gather.1
  85.1 211.0 all-reduce.3
  314.8 45.5 all-reduce.5
  363.0 106.5 reduce-scatter.4
  472.0 105.2 reduce-scatter.2
where the time goes:
time: 596 us; the launch traced here: 595 us
  waiting for transfers between devices  470 us (79%)
  local copies, waits for them, and re-layouts  40.7 us (7%)
  matrix products  32.8 us (6%)
  other arithmetic  18.6 us (3%)
  blocking collectives  18.2 us (3%)
  between operations  13.8 us (2%)
    psum x1, waiting for transfers between devices, reconstruct(): recon = lax.psum(partial_value, 'lat')  195 us
    reduce_scatter x1, waiting for transfers between devices, shards(): lax.psum_scatter(jnp.einsum('rld,rf->dlf', inputs_bf, grad_pre, preferred...  91.9 us
    reduce_scatter x1, waiting for transfers between devices, shards(): lax.psum_scatter(dec_term, 'dp', scatter_dimension=2, tiled=True)  91.6 us
    all_gather x1, waiting for transfers between devices, shards(): weight = lax.all_gather(dec_weight, 'dp', axis=2, tiled=True)  69.1 us
    unnamed x9, local copies, waits for them, and re-layouts  25.5 us
    psum x1, waiting for transfers between devices, shards(): grad_sum = lax.psum(grad_part, 'lyr')  22 us
    mul x3, local copies, waits for them, and re-layouts, dequantize(): code_block.astype(jnp.float32)  15.3 us
  transfers between devices with their start and end apart: 5, of which 5 were waited for; matrix products, arithmetic and copies ran while one was open for 9% of the time, Pallas kernels for 0%

commit v1 on v0

v1 whole, which is shorter than its diff:
```python
import jax
import jax.numpy as jnp
from jax import lax
from jax.sharding import PartitionSpec as P

penalty = 1.0
epsilon = 1e-06


def dequantize(code_block, scale_block):
    rows, width = code_block.shape
    blocks = scale_block.shape[1]
    scaled = (
        code_block.astype(jnp.float32).reshape(rows, blocks, width // blocks)
        * scale_block.astype(jnp.float32)[..., None]
    )
    return scaled.reshape(rows, width)


def swap_halves(block, half):
    width = block.shape[1] // 2
    kept = lax.dynamic_slice_in_dim(block, half * width, width, 1)
    given = lax.dynamic_slice_in_dim(block, (1 - half) * width, width, 1)
    got = lax.ppermute(given, "dp", [(0, 1), (1, 0)])
    first = jnp.where(half == 0, kept, got)
    second = jnp.where(half == 0, got, kept)
    return jnp.concatenate([first, second], axis=0)


def shards(act_codes, act_scales, latents, dec_weight, dec_bias):
    half = lax.axis_index("dp")
    lat_id = lax.axis_index("lat")
    weight = dec_weight[:, 0, :]
    width = weight.shape[1]
    wide = weight.astype(jnp.float32)
    acts = lax.all_gather(latents, "dp", axis=0, tiled=True)
    codes = swap_halves(act_codes[:, 0, :], half)
    scales = swap_halves(act_scales[:, 0, :], half)
    bias = lax.dynamic_slice_in_dim(dec_bias, half * width, width, 1)

    partial_value = jnp.dot(acts, weight, preferred_element_type=jnp.float32)
    recon = lax.psum_scatter(partial_value, "lat", scatter_dimension=0, tiled=True)
    part = recon.shape[0]
    my_inputs = dequantize(
        lax.dynamic_slice_in_dim(codes, lat_id * part, part, 0),
        lax.dynamic_slice_in_dim(scales, lat_id * part, part, 0),
    )
    resid_part = (recon + bias - my_inputs).astype(jnp.bfloat16)
    resid = lax.all_gather(resid_part, "lat", axis=0, tiled=True)

    squares = lax.psum(jnp.sum(jnp.square(wide), axis=1), "dp")
    row_norms = jnp.sqrt(squares + epsilon)
    norm_total = lax.psum(row_norms, "lyr")
    act_sum = jnp.sum(acts.astype(jnp.float32), axis=0)

    grad_part = jnp.dot(resid, weight.T, preferred_element_type=jnp.float32)
    grad_sum = lax.psum_scatter(grad_part, ("lyr", "dp"), scatter_dimension=0, tiled=True)
    rows = grad_sum.shape[0]
    place = lax.axis_index("lyr") * 2 + half
    my_acts = lax.dynamic_slice_in_dim(acts, place * rows, rows, 0)
    pre_part = jnp.where(my_acts > 0, grad_sum + penalty * norm_total[None, :], 0.0).astype(
        jnp.bfloat16
    )
    grad_pre = lax.all_gather(pre_part, ("lyr", "dp"), axis=0, tiled=True)

    scaled_rows = (penalty * act_sum / row_norms)[:, None] * wide
    grad_dec = (
        lax.dot_general(acts, resid, (((0,), (0,)), ((), ())), preferred_element_type=jnp.float32)
        + scaled_rows
    )
    inputs_bf = dequantize(codes, scales).astype(jnp.bfloat16)
    grad_enc = lax.dot_general(
        inputs_bf, grad_pre, (((0,), (0,)), ((), ())), preferred_element_type=jnp.float32
    )
    grad_bias = jnp.sum(grad_pre.astype(jnp.float32), axis=0)
    return (grad_enc[:, None, :], grad_dec[:, None, :], grad_bias)


def solution(mesh):
    in_specs = (
        P("dp", "lyr", None),
        P("dp", "lyr", None),
        P("dp", "lat"),
        P("lat", "lyr", "dp"),
        P("lyr", None),
    )
    out_specs = (P("dp", "lyr", "lat"), P("lat", "lyr", "dp"), P("lat"))
    return jax.shard_map(shards, mesh=mesh, in_specs=in_specs, out_specs=out_specs, check_vma=False)
```

time: 596 us -> 498 us (0.84)
  waiting for transfers between devices: 470 us -> 395 us
  local copies, waits for them, and re-layouts: 40.7 us -> 31 us
  other arithmetic: 18.6 us -> 11.5 us
    psum x2 -> x0, waiting for transfers between devices: 217 us -> none  [the longest x1 195 us: reconstruct(): recon = lax.psum(partial_value, 'lat')]
    all_gather x1 -> x3, waiting for transfers between devices: 69.1 us -> 140 us  [the longest x1 83 us: shards(): resid = lax.all_gather(resid_part, 'lat', axis=0, tiled=True)]
    ppermute x0 -> x2, waiting for transfers between devices: none -> 45.5 us  [swap_halves(): got = lax.ppermute(given, 'dp', [(0, 1), (1, 0)])]
    reduce_scatter x2, waiting for transfers between devices: 183 us -> 209 us  [the longest x1 169 us: shards(): lax.psum_scatter(partial_value, 'lat', scatter_dimension=0, tiled=True)]
    mul x3 -> x2, local copies, waits for them, and re-layouts: 15.3 us -> 2.41 us  [dequantize(): code_block.astype(jnp.float32).reshape(rows, blocks, width // blocks)]
    another operation x1 -> x0, other arithmetic: 11.7 us -> none
    psum x3 -> x2, blocking collectives: 18.2 us -> 15.1 us  [the longest x1 9.81 us: shards(): norm_total = lax.psum(row_norms, 'lyr')]
    unnamed x9 -> x13, local copies, waits for them, and re-layouts: 25.5 us -> 26.6 us
  transfers between devices with their start and end apart: 5 -> 7, of which waited for: 5 -> 6; matrix products, arithmetic and copies ran while one was open for 9% -> 6% of each run, Pallas kernels for 0% -> 0%
where the time goes in v1:
time: 498 us; the launch traced here: 497 us
  waiting for transfers between devices  395 us (79%)
  local copies, waits for them, and re-layouts  31 us (6%)
  matrix products  27.3 us (5%)
  blocking collectives  15.1 us (3%)
  between operations  13.9 us (3%)
  other arithmetic  11.5 us (2%)
    reduce_scatter x1, waiting for transfers between devices, shards(): lax.psum_scatter(partial_value, 'lat', scatter_dimension=0, tiled=True)  169 us
    all_gather x1, waiting for transfers between devices, shards(): resid = lax.all_gather(resid_part, 'lat', axis=0, tiled=True)  83 us
    ppermute x2, waiting for transfers between devices, swap_halves(): got = lax.ppermute(given, 'dp', [(0, 1), (1, 0)])  45.5 us
    reduce_scatter x1, waiting for transfers between devices, shards(): lax.psum_scatter(grad_part, ('lyr', 'dp'), scatter_dimension=0, tiled=True)  39.6 us
    all_gather x1, waiting for transfers between devices, shards(): acts = lax.all_gather(latents, 'dp', axis=0, tiled=True)  33.6 us
    unnamed x13, local copies, waits for them, and re-layouts  26.6 us
    all_gather x1, waiting for transfers between devices, shards(): grad_pre = lax.all_gather(pre_part, ('lyr', 'dp'), axis=0, tiled=True)  23.3 us
  transfers between devices with their start and end apart: 7, of which 6 were waited for; matrix products, arithmetic and copies ran while one was open for 6% of the time, Pallas kernels for 0%

profile of v1, /device:TPU:1, one launch (start us, length us, event | category | flops | bytes accessed | tf_op | source)
XLA Modules:
  0.0 497.1 jit_solution(17781423220486389334)
XLA Ops:
  7.2 0.7 all-gather.4.cloned.1.call-update
  8.0 33.6 %all-gather.4.cloned.1.call-done = bf16[1024,512]{1,0:T(8,128)(2,1)} async-done(((bf16[512,512]{1,0:T(8,128)(2,1)}), bf16[1024,512]{1,0:T(8,128)(2,1)}) %all-gather.4.cloned.1.call-update) | async-done | bytes 1048592 | tf_op jit(solution)/shard_map/all_gather | solution.py:36
  41.6 7.5 %fusion.11 = f32[1024,2048]{1,0:T(8,128)} fusion(bf16[1024,512]{1,0:T(8,128)(2,1)} %all-gather.4.cloned.1.call-done, bf16[512,1,2048]{2,0,1:T(8,128)(2,1)} %param.8), kind=kOutput, calls=%fused_computation.14 | convolution fusion | flops 2147483648 | bytes 11534336 | tf_op jit(solution)/shard_map/dot_general | solution.py:41
  49.1 1.7 dynamic-slice_bitcast_fusion
  50.9 0.1 collective-permute-start
  51.0 2.9 collective-permute-start.1
  53.9 45.5 %collective-permute-done.1 = bf16[512,16]{0,1:T(8,128)(2,1)S(1)} collective-permute-done((bf16[512,16]{0,1:T(8,128)(2,1)S(1)}, bf16[512,16]{0,1:T(8,128)(2,1)S(1)}, u32[]{:S(2)}, u32[]{:S(2)}) %collective-permute-start.1) | collective-permute-done | bytes 16416 | tf_op jit(solution)/shard_map/ppermute | solution.py:24
  99.4 0.1 fusion.18
  99.5 0.1 copy.17
  99.6 4.8 bitcast_select_fusion
  104.4 169.4 %reduce-scatter.3.cloned.1.call-done = f32[32,2048]{1,0:T(8,128)} async-done(((f32[1024,2048]{1,0:T(8,128)}), f32[32,2048]{1,0:T(8,128)}) %reduce-scatter.3.cloned.1.call-update) | async-done | bytes 262160 | tf_op jit(solution)/shard_map/reduce_scatter | solution.py:42
  273.8 0.1 mul.63
  274.0 1.8 fusion.14
  275.8 0.0 reduce-scatter.5.cloned.1.call-start
  275.9 83.0 %all-gather.6.cloned.1.call-done = bf16[1024,2048]{1,0:T(8,128)(2,1)} async-done(((bf16[32,2048]{1,0:T(8,128)(2,1)}), bf16[1024,2048]{1,0:T(8,128)(2,1)}) %all-gather.6.cloned.1.call-update) | async-done | bytes 4194320 | tf_op jit(solution)/shard_map/all_gather | solution.py:49
  358.8 6.5 %fusion.9 = f32[1024,512]{1,0:T(8,128)} fusion(bf16[1024,2048]{1,0:T(8,128)(2,1)} %all-gather.6.cloned.1.call-done, bf16[512,1,2048]{2,0,1:T(8,128)(2,1)} %param.8), kind=kOutput, calls=%fused_computation.12 | convolution fusion | flops 2147483648 | bytes 8388608 | tf_op jit(solution)/shard_map/dot_general | solution.py:56
  365.4 0.0 all-gather.8.cloned.1.call-start
  365.4 4.0 copy.16
  369.4 2.1 fusion.1
  371.5 5.3 %psum.14 = f32[512]{0:T(512)S(1)} all-reduce(f32[512]{0:T(512)S(1)} %fusion.1), channel_id=1, replica_groups=mesh['lat'=32,'lyr'=4,'dp'=2] {'dp'}, use_global_device_ids=true, to_apply=%region_3.4 | all-reduce | flops 512 | bytes 4096 | tf_op jit(solution)/shard_map/psum | solution.py:51
  376.8 0.2 convert_reduce_fusion.1
  377.1 9.8 %psum.15 = f32[512]{0:T(512)S(1)} all-reduce(f32[512]{0:T(512)S(1)} %get-tuple-element.14), channel_id=1, replica_groups=mesh['lat'=32,'lyr'=4,'dp'=2] {'lyr'}, use_global_device_ids=true, to_apply=%region_4.5 | all-reduce | flops 512 | bytes 4096 | tf_op jit(solution)/shard_map/psum | solution.py:53
  386.9 39.6 %reduce-scatter.5.cloned.1.call-done = f32[128,512]{1,0:T(8,128)} async-done(((f32[1024,512]{1,0:T(8,128)}), f32[128,512]{1,0:T(8,128)}) %reduce-scatter.5.cloned.1.call-update) | async-done | bytes 262160 | tf_op jit(solution)/shard_map/reduce_scatter | solution.py:57
  426.4 1.6 select_convert_fusion
  428.1 0.2 copy.15
  428.3 7.6 %fusion.3 = f32[512,1,2048]{0,2,1:T(8,128)} fusion(bf16[1024,2048]{1,0:T(8,128)(2,1)} %all-gather.6.cloned.1.call-done, bf16[1024,512]{1,0:T(8,128)(2,1)} %all-gather.4.cloned.1.call-done, bf16[512,1,2048]{0,2,1:T(8,128)(2,1)} %copy.16, f32[512]{0:T(512)S(1)} %get-tuple-element.13), kind=kOutput, calls=%fused_computation.9 | convolution fusion | flops 2150629376 | bytes 11536384 | tf_op jit(solution)/shard_map/dot_general | solution.py:68
  436.0 10.9 %copy.19 = f32[512,1,2048]{2,1,0:T(1,128)} copy(f32[512,1,2048]{0,2,1:T(8,128)} %fusion.3) | data formatting | bytes 8388608
  446.8 23.3 %all-gather.8.cloned.1.call-done = bf16[1024,512]{1,0:T(8,128)(2,1)} async-done(((bf16[128,512]{1,0:T(8,128)(2,1)}), bf16[1024,512]{1,0:T(8,128)(2,1)}) %all-gather.8.cloned.1.call-update) | async-done | bytes 1048592 | tf_op jit(solution)/shard_map/all_gather | solution.py:64
  470.1 2.3 mul.57
  472.4 5.7 %fusion.6 = f32[2048,1,512]{2,0,1:T(8,128)S(1)} fusion(bf16[1024,512]{1,0:T(8,128)(2,1)S(1)} %copy-done.3, f32[128,8,16,128]{3,2,1,0:T(8,128)S(1)} %bitcast.46, bf16[512,2048]{1,0:T(8,128)(2,1)S(1)} %get-tuple-element.9, bf16[512,2048]{1,0:T(8,128)(2,1)S(1)} %copy-done.1), kind=kOutput, calls=%fused_computation.11 | convolution fusion | flops 2160066560 | bytes 17825792 | tf_op jit(solution)/shard_map/dot_general | solution.py:72
  478.1 11.7 %copy.18 = f32[2048,1,512]{2,1,0:T(1,128)} copy(f32[2048,1,512]{2,0,1:T(8,128)S(1)} %fusion.6) | data formatting | bytes 8388608
  489.8 0.8 convert_reduce_fusion
  (23 shorter events, 0.3 us)
Async XLA Ops:
  7.2 46.8 %copy-start = (f32[1,4096]{1,0:T(1,128)S(1)}, f32[1,4096]{1,0:T(1,128)}, u32[]{:S(2)}) copy-start(f32[1,4096]{1,0:T(1,128)} %param.9) | copy-start | bytes 49156
  7.2 34.4 %all-gather.4.cloned.1.call-start = ((), (), s32[]{:S(2)}) async-start(), calls=%async_computation.2 | async-start | bytes 1572864 | tf_op jit(solution)/shard_map/all_gather | solution.py:36
  7.9 265.9 %reduce-scatter.3.cloned.1.call-start = ((), (), s32[]{:S(2)}) async-start(), calls=%async_computation.3 | async-start | bytes 8650752 | tf_op jit(solution)/shard_map/reduce_scatter | solution.py:42
  49.1 1.9 copy-start.4
  49.1 309.7 %all-gather.6.cloned.1.call-start = ((), (), s32[]{:S(2)}) async-start(), calls=%async_computation.4 | async-start | bytes 4325376 | tf_op jit(solution)/shard_map/all_gather | solution.py:49
  50.9 48.7 %collective-permute-start = (bf16[512,2048]{1,0:T(8,128)(2,1)S(1)}, bf16[512,2048]{1,0:T(8,128)(2,1)}, u32[]{:S(2)}, u32[]{:S(2)}) collective-permute-start(bf16[512,2048]{1,0:T(8,128)(2,1)S(1)} %dynamic-slice_bitcast_fusion), channel_id=1, source_target_pairs={{0,1},{1,0},{2,3},{3,2},{4,5},{5,4},{6,7},{7,6},{8,9},{9,8},{10,11... | collective-permute-start | bytes 6291464 | tf_op jit(solution)/shard_map/ppermute | solution.py:24
  51.0 48.4 %collective-permute-start.1 = (bf16[512,16]{0,1:T(8,128)(2,1)S(1)}, bf16[512,16]{0,1:T(8,128)(2,1)S(1)}, u32[]{:S(2)}, u32[]{:S(2)}) collective-permute-start(bf16[512,16]{0,1:T(8,128)(2,1)S(1)} %dynamic-slice_bitcast_fusion.1), channel_id=1, source_target_pairs={{0,1},{1,0},{2,3},{3,2},{4,5},{5,4},{6,7},{7,6},{8,9},{9,8},{10,11... | collective-permute-start | bytes 49160 | tf_op jit(solution)/shard_map/ppermute | solution.py:24
  275.8 150.6 %reduce-scatter.5.cloned.1.call-start = ((), (), s32[]{:S(2)}) async-start(), calls=%async_computation.5 | async-start | bytes 2359296 | tf_op jit(solution)/shard_map/reduce_scatter | solution.py:57
  365.4 11.5 %copy-start.2 = (bf16[1024,512]{1,0:T(8,128)(2,1)S(1)}, bf16[1024,512]{1,0:T(8,128)(2,1)}, u32[]{:S(2)}) copy-start(bf16[1024,512]{1,0:T(8,128)(2,1)} %all-gather.4.cloned.1.call-done) | copy-start | bytes 3145732
  365.4 104.7 %all-gather.8.cloned.1.call-start = ((), (), s32[]{:S(2)}) async-start(), calls=%async_computation.6 | async-start | bytes 1179648 | tf_op jit(solution)/shard_map/all_gather | solution.py:64
  470.1 2.3 copy-start.1
  470.1 2.3 copy-start.3
Sparse Core Ops, SparseCore 0:
  9.8 31.7 all-gather.3
  49.2 224.6 reduce-scatter.2
  277.3 81.4 all-gather.5
  365.5 60.8 reduce-scatter.4
  428.2 41.8 all-gather.7

commit v2 on v0

v2 whole, which is shorter than its diff:
```python
import functools

import jax
import jax.numpy as jnp
from jax import lax
from jax.experimental import pallas as pl
from jax.experimental.pallas import tpu as pltpu
from jax.sharding import PartitionSpec as P

penalty = 1.0
epsilon = 1e-06
MESH = pl.DeviceIdType.MESH
f32, bf16 = jnp.float32, jnp.bfloat16

ROWS, FB, WIDTH = 1024, 512, 2048
HALF = WIDTH // 2
PIECE = HALF // 4
NT = (((1,), (1,)), ((), ()))
TN = (((0,), (0,)), ((), ()))


def aligned(value, step):
    return pl.multiple_of(value, step)


def spread(scales, first, width):
    blocks = scales.shape[0]
    row = lax.broadcasted_iota(jnp.int32, (blocks, width), 0)
    col = lax.broadcasted_iota(jnp.int32, (blocks, width), 1)
    pick = jnp.where(row == first + col // 128, 1.0, 0.0).astype(bf16)
    return lax.dot_general(scales, pick, TN, preferred_element_type=f32)


def exchange_kernel(
    lat, w, sc, bias, codes,
    resid_o, acts_o, pre_o, sq_o, codes_o, sc_o,
    la, wx, part, rs, resid, grad, grad_in, grad_y, pre, mine_codes, other_codes, sq_mine, sq_other, sc_other,
    local_sem, l1s, l1r, wss, wsr, l2s, l2r, l3s, l3r, rss, rsr, xs_, xr_, z0s, z0r, z1s, z1r, x1s, x1r,
    gcs, gcr, gys, gyr, pys, pyr, pcs, pcr, ms, mr, cs, cr,
):
    lat_id = lax.axis_index("lat")
    lyr = lax.axis_index("lyr")
    h = lax.axis_index("dp")
    x, z = lat_id % 4, lat_id // 4
    ylo, c = lyr // 2, lyr % 2
    y = h * 2 + ylo

    def at(xx=x, yy=y, zz=z, cc=c):
        return (zz * 4 + xx, (yy % 2) * 2 + cc, yy // 2)

    xp = [(x + o) % 4 for o in range(4)]
    yp = [(y + o) % 4 for o in range(4)]
    zr, zl = (z + 1) % 8, (z + 7) % 8
    sibling = at(cc=1 - c)
    partner = at(yy=yp[2])

    def rcopy(src, dst, send, recv, device):
        return pltpu.make_async_remote_copy(
            src_ref=src, dst_ref=dst, send_sem=send, recv_sem=recv, device_id=device, device_id_type=MESH
        )

    barrier = pltpu.get_barrier_semaphore()
    neighbours = [at(xx=xp[o]) for o in (1, 2, 3)] + [at(yy=yp[o]) for o in (1, 2, 3)]
    neighbours += [at(zz=zr), at(zz=zl), sibling]
    for d in neighbours:
        pl.semaphore_signal(barrier, inc=1, device_id=d, device_id_type=MESH)
    pl.semaphore_wait(barrier, len(neighbours))

    sends = []
    my_block = aligned((y * 2 + c) * 128, 128)
    my_cols = aligned(x * FB, FB)

    own = aligned((ylo * 2 + c) * 128, 128)
    l1 = []
    for o in (1, 2, 3):
        cp = rcopy(
            lat.at[pl.ds(own, 128), :],
            la.at[pl.ds(my_block, 128), pl.ds(my_cols, FB)],
            l1s.at[o - 1], l1r.at[o - 1], at(xx=xp[o]),
        )
        cp.start()
        l1.append(cp)
    wcopies = [[], []]
    for k in range(2):
        for o in (1, 2, 3):
            cols = aligned(k * HALF + xp[o] * PIECE, PIECE)
            cp = rcopy(
                w.at[:, pl.ds(cols, PIECE)],
                wx.at[k, pl.ds(my_cols, FB), :],
                wss.at[k, o - 1], wsr.at[k, o - 1], at(xx=xp[o]),
            )
            cp.start()
            wcopies[k].append(cp)
    row0 = aligned((z % 4) * 128, 128)
    misc = []
    for k in range(2):
        theirs = aligned((1 - h) * WIDTH + k * HALF + x * PIECE, PIECE)
        cp = rcopy(codes.at[pl.ds(row0, 128), pl.ds(theirs, PIECE)], other_codes.at[k], ms.at[k], mr.at[k], partner)
        cp.start()
        misc.append(cp)
        ours = aligned(h * WIDTH + k * HALF + x * PIECE, PIECE)
        cp = pltpu.make_async_copy(
            codes.at[pl.ds(row0, 128), pl.ds(ours, PIECE)], mine_codes.at[k], local_sem.at[k]
        )
        cp.start()
        misc.append(cp)
    cp = rcopy(sc.at[pl.ds(aligned((1 - h) * 16, 16), 16), :], sc_other, ms.at[2], mr.at[2], partner)
    cp.start()
    misc.append(cp)

    la[pl.ds(my_block, 128), pl.ds(my_cols, FB)] = lat[pl.ds(own, 128), :]
    for k in range(2):
        cols = aligned(k * HALF + x * PIECE, PIECE)
        wx[k, pl.ds(my_cols, FB), :] = w[:, pl.ds(cols, PIECE)]

    ones = jnp.ones((8, WIDTH), bf16)

    @pl.loop(0, 4)
    def _(i):
        at_f = aligned(i * 128, 128)
        wide = w[pl.ds(at_f, 128), :].astype(f32)
        square = wide * wide
        high = square.astype(bf16)
        low = (square - high.astype(f32)).astype(bf16)
        sq_mine[:, pl.ds(at_f, 128)] = lax.dot_general(
            ones, high, NT, preferred_element_type=f32
        ) + lax.dot_general(ones, low, NT, preferred_element_type=f32)

    cp = rcopy(sq_mine, sq_other, ms.at[3], mr.at[3], partner)
    cp.start()
    misc.append(cp)

    for cp in l1:
        cp.wait_recv()
    l2 = {}
    block = la.at[pl.ds(my_block, 128), :]
    l3 = []
    cp = rcopy(block, block, l3s.at[0], l3r.at[0], sibling)
    cp.start()
    l3.append(cp)
    for o in (1, 3, 2):
        cp = rcopy(block, block, l2s.at[o - 1], l2r.at[o - 1], at(yy=yp[o]))
        cp.start()
        l2[o] = cp

    def dots(chunk, k):
        rows = aligned(chunk * 256, 256)
        part[k, pl.ds(rows, 256), :] = jnp.dot(
            la[pl.ds(rows, 256), :], wx[k], preferred_element_type=f32
        )

    l3[0].wait_recv()
    for k in range(2):
        for cp in wcopies[k]:
            cp.wait_recv()

    @pl.loop(0, 2)
    def _(k):
        dots(y, k)

    for i, o in enumerate((3, 1, 2)):
        source = (y + 4 - o) % 4
        l2[o].wait_recv()
        arrived = la.at[pl.ds(aligned((source * 2 + c) * 128, 128), 128), :]
        cp = rcopy(arrived, arrived, l3s.at[i + 1], l3r.at[i + 1], sibling)
        cp.start()
        l3.append(cp)
        cp.wait_recv()

        @pl.loop(0, 2)
        def _(k, source=source):
            dots(source, k)

    code_copies = []
    theirs = aligned((1 - h) * WIDTH, WIDTH)
    for i in range(4):
        cp = rcopy(
            codes.at[pl.ds(i * 128, 128), pl.ds(theirs, WIDTH)],
            codes_o.at[pl.ds(i * 128, 128), :],
            cs.at[i], cr.at[i], partner,
        )
        cp.start()
        code_copies.append(cp)

    def local_part(k, s, owner):
        return part[k, pl.ds(aligned(owner * 128 + s * 64, 64), 64), :]

    def ring_owner(s, step):
        return (z + 15 - step) % 8 if s == 0 else (z + 1 + step) % 8

    ring = {}
    for k in range(2):
        for s in range(2):
            cp = rcopy(
                part.at[k, pl.ds(aligned(ring_owner(s, 0) * 128 + s * 64, 64), 64), :],
                rs.at[k, s, 0], rss.at[k, s, 0], rsr.at[k, s, 0], at(zz=zr if s == 0 else zl),
            )
            cp.start()
            ring[k, s, 0] = cp
    for step in range(1, 7):
        for k in range(2):
            for s in range(2):
                ring[k, s, step - 1].wait_recv()
                rs[k, s, step - 1] += local_part(k, s, ring_owner(s, step))
                cp = rcopy(
                    rs.at[k, s, step - 1], rs.at[k, s, step],
                    rss.at[k, s, step], rsr.at[k, s, step], at(zz=zr if s == 0 else zl),
                )
                cp.start()
                ring[k, s, step] = cp

    for cp in misc:
        cp.wait()
    is_own = (z // 4) == h
    my_scales = jnp.where(
        is_own,
        sc[pl.ds(aligned(h * 16, 16), 16), pl.ds(row0, 128)].astype(f32),
        sc_other[:, pl.ds(row0, 128)].astype(f32),
    ).astype(bf16)
    x_cols = aligned(x * PIECE, PIECE)
    z_rows = aligned(z * 128, 128)
    x0, x1 = [], {}
    for k in range(2):
        wide_codes = jnp.where(is_own, mine_codes[k].astype(f32), other_codes[k].astype(f32))
        inputs = wide_codes * spread(my_scales, k * 8 + x * 2, PIECE)
        shift = bias[:, pl.ds(aligned(h * WIDTH + k * HALF + x * PIECE, PIECE), PIECE)]
        for s in range(2):
            ring[k, s, 6].wait_recv()
            recon = rs[k, s, 6] + local_part(k, s, z)
            value = (recon + shift - inputs[s * 64 : s * 64 + 64, :]).astype(bf16)
            resid[k, pl.ds(aligned(z * 128 + s * 64, 64), 64), pl.ds(x_cols, PIECE)] = value
        if k == 0:
            tile = resid.at[0, pl.ds(z_rows, 128), pl.ds(x_cols, PIECE)]
            for o in (1, 2, 3):
                cp = rcopy(tile, tile, xs_.at[o - 1], xr_.at[o - 1], at(xx=xp[o]))
                cp.start()
                x0.append(cp)

    def send_z(k, sems, rows, count, step, way):
        cols = pl.ds(0, HALF) if k == 0 else pl.ds(x_cols, PIECE)
        tile = resid.at[k, pl.ds(rows, count), cols]
        cp = rcopy(tile, tile, sems[0].at[way, step], sems[1].at[way, step], at(zz=zr if way == 0 else zl))
        cp.start()
        return cp

    def send_x1(owner, index):
        tile = resid.at[1, pl.ds(aligned(owner * 128, 128), 128), pl.ds(x_cols, PIECE)]
        out = []
        for o in (1, 2, 3):
            cp = rcopy(tile, tile, x1s.at[index, o - 1], x1r.at[index, o - 1], at(xx=xp[o]))
            cp.start()
            out.append(cp)
        return out

    squares = sq_mine[0:1, :] + sq_other[0:1, :]
    sq_o[...] = jnp.broadcast_to(squares, sq_o.shape)
    half_norms = (0.5 * penalty) * jnp.sqrt(squares + epsilon)

    def grad_rows(first, count):
        rows = pl.ds(aligned(first, count), count)
        grad[rows, :] = (
            lax.dot_general(resid[0, rows, :], w[:, :HALF], NT, preferred_element_type=f32)
            + lax.dot_general(resid[1, rows, :], w[:, HALF:], NT, preferred_element_type=f32)
            + half_norms
        )

    zc = {}
    zc[1, 0, 0] = send_z(1, (z1s, z1r), z_rows, 128, 0, 0)
    zc[1, 1, 0] = send_z(1, (z1s, z1r), z_rows, 128, 0, 1)
    x1[0] = send_x1(z, 0)
    for cp in x0:
        cp.wait_recv()
    zc[0, 0, 0] = send_z(0, (z0s, z0r), z_rows, 128, 0, 0)
    zc[0, 1, 0] = send_z(0, (z0s, z0r), z_rows, 128, 0, 1)
    for cp in x1[0]:
        cp.wait_recv()
    grad_rows(z * 128, 128)
    for step in range(1, 5):
        for way in range(2):
            source = (z + 8 - step) % 8 if way == 0 else (z + step) % 8
            rows = aligned(source * 128, 128)
            count = 128
            if step == 4:
                rows, count = aligned(source * 128 + way * 64, 64), 64
            for k, sems in ((1, (z1s, z1r)), (0, (z0s, z0r))):
                zc[k, way, step - 1].wait_recv()
                if step < 3:
                    zc[k, way, step] = send_z(k, sems, rows, 128, step, way)
                elif step == 3:
                    zc[k, way, step] = send_z(k, sems, aligned(source * 128 + way * 64, 64), 64, step, way)
                if k == 1 and step < 4:
                    x1[step * 2 - 1 + way] = send_x1(source, step * 2 - 1 + way)
            if step < 4:
                for cp in x1[step * 2 - 1 + way]:
                    cp.wait_recv()
                grad_rows(source * 128, 128)
    x1[7] = send_x1((z + 4) % 8, 7)
    for cp in x1[7]:
        cp.wait_recv()
    grad_rows(((z + 4) % 8) * 128, 128)

    out_copies = [
        pltpu.make_async_copy(resid, resid_o, local_sem.at[2]),
        pltpu.make_async_copy(la.at[:, pl.ds(my_cols, FB)], acts_o, local_sem.at[3]),
    ]
    for cp in out_copies:
        cp.start()

    gc = []
    for o in (2, 1, 3, 0):
        rows = pl.ds(aligned((yp[o] * 2 + 1 - c) * 128, 128), 128)
        cp = rcopy(grad.at[rows, :], grad_in.at[o], gcs.at[o], gcr.at[o], sibling)
        cp.start()
        gc.append((o, cp))
    gy = []
    for o, cp in gc:
        cp.wait_recv()
        rows = pl.ds(aligned((yp[o] * 2 + c) * 128, 128), 128)
        grad_in[o] = grad_in[o] + grad[rows, :]
        if o:
            out = rcopy(grad_in.at[o], grad_y.at[o - 1], gys.at[o - 1], gyr.at[o - 1], at(yy=yp[o]))
            out.start()
            gy.append(out)
    total = grad_in[0]
    for cp in gy:
        cp.wait_recv()
    total = total + grad_y[0] + grad_y[1] + grad_y[2]
    active = la[pl.ds(my_block, 128), pl.ds(my_cols, FB)].astype(f32) > 0
    pre[pl.ds(my_block, 128), :] = jnp.where(active, total, 0.0).astype(bf16)
    tile = pre.at[pl.ds(my_block, 128), :]
    pc = [rcopy(tile, tile, pcs.at[0], pcr.at[0], sibling)]
    pc[0].start()
    py = {}
    for o in (2, 1, 3):
        py[o] = rcopy(tile, tile, pys.at[o - 1], pyr.at[o - 1], at(yy=yp[o]))
        py[o].start()
    for i, o in enumerate((1, 3, 2)):
        py[o].wait_recv()
        source = (y + 4 - o) % 4
        tile = pre.at[pl.ds(aligned((source * 2 + c) * 128, 128), 128), :]
        cp = rcopy(tile, tile, pcs.at[i + 1], pcr.at[i + 1], sibling)
        cp.start()
        pc.append(cp)
    for cp in pc:
        cp.wait_recv()
    pre_o[...] = pre[...]
    sc_o[...] = sc_other[...]

    for cp in code_copies:
        cp.wait()
    for cp in out_copies:
        cp.wait()
    for cp in l1 + wcopies[0] + wcopies[1] + list(l2.values()) + l3 + list(ring.values()) + x0:
        cp.wait_send()
    for cp in list(zc.values()) + sum(x1.values(), []) + [cp for _, cp in gc] + gy + list(py.values()) + pc:
        cp.wait_send()


def exchange(lat, w, sc, bias, codes):
    vmem = pl.BlockSpec(memory_space=pltpu.VMEM)
    hbm = pl.BlockSpec(memory_space=pl.ANY)
    dma = pltpu.SemaphoreType.DMA
    shape = jax.ShapeDtypeStruct
    return pl.pallas_call(
        exchange_kernel,
        out_shape=[
            shape((2, ROWS, HALF), bf16),
            shape((ROWS, FB), bf16),
            shape((ROWS, FB), bf16),
            shape((8, FB), f32),
            shape((ROWS // 2, WIDTH), bf16),
            shape((16, ROWS // 2), bf16),
        ],
        in_specs=[vmem, vmem, vmem, vmem, hbm],
        out_specs=[hbm, hbm, vmem, vmem, hbm, vmem],
        scratch_shapes=[
            pltpu.VMEM((ROWS, 4 * FB), bf16),
            pltpu.VMEM((2, 4 * FB, PIECE), bf16),
            pltpu.VMEM((2, ROWS, PIECE), f32),
            pltpu.VMEM((2, 2, 7, 64, PIECE), f32),
            pltpu.VMEM((2, ROWS, HALF), bf16),
            pltpu.VMEM((ROWS, FB), f32),
            pltpu.VMEM((4, 128, FB), f32),
            pltpu.VMEM((3, 128, FB), f32),
            pltpu.VMEM((ROWS, FB), bf16),
            pltpu.VMEM((2, 128, PIECE), bf16),
            pltpu.VMEM((2, 128, PIECE), bf16),
            pltpu.VMEM((8, FB), f32),
            pltpu.VMEM((8, FB), f32),
            pltpu.VMEM((16, ROWS // 2), bf16),
            dma((4,)),
            dma((3,)), dma((3,)),
            dma((2, 3)), dma((2, 3)),
            dma((3,)), dma((3,)),
            dma((4,)), dma((4,)),
            dma((2, 2, 7)), dma((2, 2, 7)),
            dma((3,)), dma((3,)),
            dma((2, 4)), dma((2, 4)),
            dma((2, 4)), dma((2, 4)),
            dma((8, 3)), dma((8, 3)),
            dma((4,)), dma((4,)),
            dma((3,)), dma((3,)),
            dma((3,)), dma((3,)),
            dma((4,)), dma((4,)),
            dma((4,)), dma((4,)),
            dma((4,)), dma((4,)),
        ],
        compiler_params=pltpu.CompilerParams(
            collective_id=0, has_side_effects=True, vmem_limit_bytes=50 * 2**20
        ),
        name="exchange",
    )(lat, w, sc, bias, codes)


def grads_kernel(half, acts, resid, w, pre, squares, own_codes, other_codes, own_sc, other_sc, enc_o, dec_o, bias_o):
    step = pl.program_id(0)
    h = half[0]
    act_sum = jnp.sum(acts[...].astype(f32), axis=0, keepdims=True)
    scale = penalty * act_sum / jnp.sqrt(squares[0:1, :] + epsilon)
    column = jnp.broadcast_to(scale, (128, 128)).T
    for k in range(2):
        term = lax.dot_general(acts[...], resid[k], TN, preferred_element_type=f32)
        for j in range(8):
            cols = slice(k * HALF + j * 128, k * HALF + j * 128 + 128)
            dec_o[pl.ds(k * 8 + j, 128, stride=16), :] = (
                term[:, j * 128 : j * 128 + 128] + column * w[:, cols].astype(f32)
            )
    own_at = pl.multiple_of(h * 512, 512)
    other_at = pl.multiple_of((1 - h) * 512, 512)
    own_in = (own_codes[...].astype(f32) * spread(own_sc[...], step * 4, 512)).astype(bf16)
    other_in = (other_codes[...].astype(f32) * spread(other_sc[...], step * 4, 512)).astype(bf16)
    enc = lax.dot_general(own_in, pre[pl.ds(own_at, 512), :], TN, preferred_element_type=f32)
    enc += lax.dot_general(other_in, pre[pl.ds(other_at, 512), :], TN, preferred_element_type=f32)
    for j in range(4):
        enc_o[pl.ds(j, 512, stride=4), :] = enc[:, j * 128 : j * 128 + 128]

    @pl.when(step == 0)
    def _():
        bias_o[...] = jnp.broadcast_to(jnp.sum(pre[...].astype(f32), axis=0, keepdims=True), bias_o.shape)


def grads(half, acts, resid, w, pre, squares, codes, other_codes, sc, other_sc):
    whole = lambda *shape: pl.BlockSpec(shape, lambda i, h: (0,) * len(shape))
    return pl.pallas_call(
        grads_kernel,
        grid_spec=pltpu.PrefetchScalarGridSpec(
            num_scalar_prefetch=1,
            grid=(4,),
            in_specs=[
                pl.BlockSpec((ROWS, 128), lambda i, h: (0, i)),
                whole(2, ROWS, HALF),
                pl.BlockSpec((128, WIDTH), lambda i, h: (i, 0)),
                whole(ROWS, FB),
                pl.BlockSpec((8, 128), lambda i, h: (0, i)),
                pl.BlockSpec((512, 512), lambda i, h: (0, h[0] * 4 + i)),
                pl.BlockSpec((512, 512), lambda i, h: (0, i)),
                pl.BlockSpec((16, 512), lambda i, h: (h[0], 0)),
                whole(16, 512),
            ],
            out_specs=[
                pl.BlockSpec((2048, 128), lambda i, h: (i, 0)),
                pl.BlockSpec((2048, 128), lambda i, h: (i, 0)),
                whole(8, FB),
            ],
        ),
        out_shape=[
            jax.ShapeDtypeStruct((WIDTH * 4, 128), f32),
            jax.ShapeDtypeStruct((FB * 16, 128), f32),
            jax.ShapeDtypeStruct((8, FB), f32),
        ],
        compiler_params=pltpu.CompilerParams(vmem_limit_bytes=50 * 2**20),
        name="grads",
    )(half, acts, resid, w, pre, squares, codes, other_codes, sc, other_sc)


def shards(act_codes, act_scales, latents, dec_weight, dec_bias):
    w = dec_weight[:, 0, :]
    codes = act_codes[:, 0, :]
    sc = act_scales[:, 0, :].T
    resid, acts, pre, squares, other_codes, other_sc = exchange(latents, w, sc, dec_bias, codes)
    half = lax.axis_index("dp").astype(jnp.int32).reshape(1)
    enc, dec, bias = grads(half, acts, resid, w, pre, squares, codes, other_codes, sc, other_sc)
    return enc.reshape(WIDTH, 1, FB), dec.reshape(FB, 1, WIDTH), bias[0]


def solution(mesh):
    in_specs = (
        P("dp", "lyr", None),
        P("dp", "lyr", None),
        P("dp", "lat"),
        P("lat", "lyr", "dp"),
        P("lyr", None),
    )
    out_specs = (P("dp", "lyr", "lat"), P("lat", "lyr", "dp"), P("lat"))
    return jax.shard_map(shards, mesh=mesh, in_specs=in_specs, out_specs=out_specs, check_vma=False)
```

time: 596 us -> 168 us (0.28)
  waiting for transfers between devices: 470 us -> 0 us
  Pallas kernels: 0 us -> 164 us
  local copies, waits for them, and re-layouts: 40.7 us -> 3.09 us
  matrix products: 32.8 us -> 0 us
  other arithmetic: 18.6 us -> 0 us
  blocking collectives: 18.2 us -> 0 us
  between operations: 13.8 us -> 0.65 us
    psum x2 -> x0, waiting for transfers between devices: 217 us -> none  [the longest x1 195 us: reconstruct(): recon = lax.psum(partial_value, 'lat')]
    reduce_scatter x2 -> x0, waiting for transfers between devices: 183 us -> none  [the longest x1 91.9 us: shards(): lax.psum_scatter(jnp.einsum('rld,rf->dlf', inputs_bf, grad_pre, preferred...]
    pallas_call x0 -> x2, Pallas kernels: none -> 164 us  [the longest x1 152 us: exchange(): pl.pallas_call(exchange_kernel, out_shape=[shape((2, ROWS, HALF), bf16),...]
    all_gather x1 -> x0, waiting for transfers between devices: 69.1 us -> none  [shards(): weight = lax.all_gather(dec_weight, 'dp', axis=2, tiled=True)]
    dot_general x4 -> x0, matrix products: 32.8 us -> none  [the longest x1 10.2 us: shards(): jnp.einsum('rld,rf->dlf', inputs_bf, grad_pre, preferred_element_type=jnp...]
    unnamed x9 -> x6, local copies, waits for them, and re-layouts: 25.5 us -> 2.51 us
    psum x3 -> x0, blocking collectives: 18.2 us -> none  [the longest x2 11.2 us: shards(): lax.psum((local_squares, jnp.sum(latents.astype(jnp.float32), axis=0)), '...]
    mul x3 -> x0, local copies, waits for them, and re-layouts: 15.3 us -> none  [dequantize(): code_block.astype(jnp.float32)]
  transfers between devices with their start and end apart: 5 -> 0, of which waited for: 5 -> 0; matrix products, arithmetic and copies ran while one was open for 9% -> 0% of each run, Pallas kernels for 0% -> 0%
where the time goes in v2:
time: 168 us
  Pallas kernels  164 us (98%)
  local copies, waits for them, and re-layouts  3.09 us (2%)
    pallas_call x1, Pallas kernels, exchange(): pl.pallas_call(exchange_kernel, out_shape=[shape((2, ROWS, HALF), bf16),...  152 us
    pallas_call x1, Pallas kernels, grads(): pl.pallas_call(grads_kernel, grid_spec=pltpu.PrefetchScalarGridSpec(num_s...  12.4 us

profile of v2, /device:TPU:1, one launch (start us, length us, event | category | flops | bytes accessed | tf_op | source)
XLA Modules:
  0.0 168.0 jit_solution(7049481445297325066)
XLA Ops:
  0.6 0.0 copy-start
  0.6 1.0 copy-done
  1.7 0.0 copy-start.1
  1.7 0.8 copy-done.1
  2.4 0.0 copy-start.2
  2.4 0.7 copy-done.2
  3.2 151.9 %exchange.1 = (bf16[2,1024,1024]{2,1,0:T(8,128)(2,1)}, bf16[1024,512]{1,0:T(8,128)(2,1)S(1)}, bf16[1024,512]{1,0:T(8,128)(2,1)S(1)}, f32[8,512]{1,0:T(8,128)S(1)...) custom-call(bf16[512,512]{1,0:T(8,128)(2,1)S(1)} %copy-done, bf16[512,2048]{1,0:T(8,128)(2,1)} %bitcast.13, ...), custom_call_target="tpu_custom_call" | custom-call | tf_op jit(solution)/shard_map/exchange/pallas_call | solution.py:364
  155.0 12.4 %grads.1 = (f32[8192,128]{1,0:T(8,128)}, f32[8192,128]{1,0:T(8,128)}, f32[8,512]{1,0:T(8,128)S(1)}) custom-call(s32[1]{0:T(128)} %bitcast.half, bf16[1024,512]{1,0:T(8,128)(2,1)S(1)} %get-tuple-element.12.acts, bf16[2,1024,1024]{2,1,0:T(8,128)(2,1)} %get-tuple-element.13.resid, bf16[512,2048]{1,0:T(8,128)(2,1)} %bitcast.14, ...), custom_call_target="tpu_custom_call" | custom-call | tf_op jit(solution)/shard_map/grads/pallas_call | solution.py:444
  167.4 0.6 slice.3
Async XLA Ops:
  0.6 1.0 copy-start
  1.7 0.8 copy-start.1
  2.4 0.7 copy-start.2

commit v3 on v0

v3 whole, which is shorter than its diff:
```python
import functools

import jax
import jax.numpy as jnp
from jax import lax
from jax.experimental import pallas as pl
from jax.experimental.pallas import tpu as pltpu
from jax.sharding import PartitionSpec as P

penalty = 1.0
epsilon = 1e-06
MESH = pl.DeviceIdType.MESH
f32, bf16 = jnp.float32, jnp.bfloat16

ROWS, FB, WIDTH = 1024, 512, 2048
HALF = WIDTH // 2
PIECE = HALF // 4
NT = (((1,), (1,)), ((), ()))
TN = (((0,), (0,)), ((), ()))


def aligned(value, step):
    return pl.multiple_of(value, step)


def spread(scales, first, width):
    blocks = scales.shape[0]
    row = lax.broadcasted_iota(jnp.int32, (blocks, width), 0)
    col = lax.broadcasted_iota(jnp.int32, (blocks, width), 1)
    pick = jnp.where(row == first + col // 128, 1.0, 0.0).astype(bf16)
    return lax.dot_general(scales, pick, TN, preferred_element_type=f32)


class Copies:
    def __init__(self):
        self.started = []

    def start(self, src, dst, sems, index, device):
        cp = pltpu.make_async_remote_copy(
            src_ref=src,
            dst_ref=dst,
            send_sem=sems[0].at[index],
            recv_sem=sems[1].at[index],
            device_id=device,
            device_id_type=MESH,
        )
        cp.start()
        self.started.append(cp)
        return cp

    def finish(self):
        for cp in self.started:
            cp.wait_send()


def exchange_kernel(
    lat, w_hbm, sc, bias, codes,
    resid_o, acts_o, pre_o, sq_o, codes_o, sc_o,
    la, w, wx, part, rs, resid, grad, core_in, core_sum, y_in, pre, mine_codes, other_codes, sq_mine, sq_other, sc_other,
    local_sem,
    l1a, l1b, wa, wb, l2a, l2b, l3a, l3b, rsa, rsb, x0a, x0b, z0a, z0b, z1a, z1b, x1a, x1b,
    gca, gcb, gya, gyb, pya, pyb, pca, pcb, ma, mb, ca, cb,
):
    lat_id = lax.axis_index("lat")
    lyr = lax.axis_index("lyr")
    h = lax.axis_index("dp")
    x, z = lat_id % 4, lat_id // 4
    ylo, c = lyr // 2, lyr % 2
    y = h * 2 + ylo

    def at(xx=x, yy=y, zz=z, cc=c):
        return (zz * 4 + xx, (yy % 2) * 2 + cc, yy // 2)

    xp = [(x + o) % 4 for o in range(4)]
    yp = [(y + o) % 4 for o in range(4)]
    z_way = [at(zz=(z + 1) % 8), at(zz=(z + 7) % 8)]
    sibling = at(cc=1 - c)
    partner = at(yy=yp[2])
    remote = Copies()

    my_block = aligned((y * 2 + c) * 128, 128)
    my_cols = aligned(x * FB, FB)
    own = aligned((ylo * 2 + c) * 128, 128)
    x_cols = aligned(x * PIECE, PIECE)
    row0 = aligned((z % 4) * 128, 128)

    w_copy = pltpu.make_async_copy(w_hbm, w, local_sem.at[0])
    w_copy.start()
    own_copies = [
        pltpu.make_async_copy(
            lat.at[pl.ds(own, 128), :], la.at[pl.ds(my_block, 128), pl.ds(my_cols, FB)], local_sem.at[1]
        )
    ]
    for k in range(2):
        own_copies.append(
            pltpu.make_async_copy(
                w_hbm.at[:, pl.ds(aligned(k * HALF + x * PIECE, PIECE), PIECE)],
                wx.at[k, pl.ds(my_cols, FB), :],
                local_sem.at[2 + k],
            )
        )
    code_parts = []
    for k in range(2):
        ours = aligned(h * WIDTH + k * HALF + x * PIECE, PIECE)
        code_parts.append(
            pltpu.make_async_copy(
                codes.at[pl.ds(row0, 128), pl.ds(ours, PIECE)], mine_codes.at[k], local_sem.at[4 + k]
            )
        )
    for cp in own_copies + code_parts:
        cp.start()

    barrier = pltpu.get_barrier_semaphore()
    neighbours = [at(xx=xp[o]) for o in (1, 2, 3)] + [at(yy=yp[o]) for o in (1, 2, 3)]
    neighbours += [z_way[0], z_way[1], sibling]
    for d in neighbours:
        pl.semaphore_signal(barrier, inc=1, device_id=d, device_id_type=MESH)
    pl.semaphore_wait(barrier, len(neighbours))

    l1 = [
        remote.start(
            lat.at[pl.ds(own, 128), :],
            la.at[pl.ds(my_block, 128), pl.ds(my_cols, FB)],
            (l1a, l1b), o - 1, at(xx=xp[o]),
        )
        for o in (1, 2, 3)
    ]
    weights = [
        [
            remote.start(
                w_hbm.at[:, pl.ds(aligned(k * HALF + xp[o] * PIECE, PIECE), PIECE)],
                wx.at[k, pl.ds(my_cols, FB), :],
                (wa, wb), (k, o - 1), at(xx=xp[o]),
            )
            for o in (1, 2, 3)
        ]
        for k in range(2)
    ]
    misc = []
    for k in range(2):
        theirs = aligned((1 - h) * WIDTH + k * HALF + x * PIECE, PIECE)
        misc.append(
            remote.start(
                codes.at[pl.ds(row0, 128), pl.ds(theirs, PIECE)], other_codes.at[k], (ma, mb), k, partner
            )
        )
    misc.append(remote.start(sc.at[pl.ds(aligned((1 - h) * 16, 16), 16), :], sc_other, (ma, mb), 2, partner))

    for cp in own_copies:
        cp.wait()
    for cp in l1:
        cp.wait_recv()
    block = la.at[pl.ds(my_block, 128), :]
    l2 = {o: remote.start(block, block, (l2a, l2b), o - 1, at(yy=yp[o])) for o in (2, 1, 3)}
    l3 = [remote.start(block, block, (l3a, l3b), 0, sibling)]

    w_copy.wait()
    ones = jnp.ones((8, WIDTH), bf16)

    @pl.loop(0, 4)
    def _(i):
        at_f = aligned(i * 128, 128)
        wide = w[pl.ds(at_f, 128), :].astype(f32)
        square = wide * wide
        high = square.astype(bf16)
        low = (square - high.astype(f32)).astype(bf16)
        sq_mine[:, pl.ds(at_f, 128)] = lax.dot_general(
            ones, high, NT, preferred_element_type=f32
        ) + lax.dot_general(ones, low, NT, preferred_element_type=f32)

    misc.append(remote.start(sq_mine, sq_other, (ma, mb), 3, partner))

    def dots(chunk, k):
        rows = aligned(chunk * 256, 256)
        part[k, pl.ds(rows, 256), :] = jnp.dot(
            la[pl.ds(rows, 256), :], wx[k], preferred_element_type=f32
        )

    def pass_on(o, index):
        l2[o].wait_recv()
        arrived = la.at[pl.ds(aligned((yp[4 - o] * 2 + c) * 128, 128), 128), :]
        l3.append(remote.start(arrived, arrived, (l3a, l3b), index, sibling))

    for cp in weights[0]:
        cp.wait_recv()
    l3[0].wait_recv()
    dots(y, 0)
    pass_on(3, 1)
    pass_on(1, 2)
    l3[1].wait_recv()
    dots(yp[1], 0)
    pass_on(2, 3)
    l3[2].wait_recv()
    dots(yp[3], 0)
    l3[3].wait_recv()
    dots(yp[2], 0)

    def local_part(k, s, u, owner):
        return pl.ds(aligned(owner * 128 + s * 64 + u * 32, 32), 32)

    def ring_owner(s, step):
        return (z + 15 - step) % 8 if s == 0 else (z + 1 + step) % 8

    streams = [(s, u) for u in range(2) for s in range(2)]
    ring = {}

    def ring_start(k):
        for s, u in streams:
            ring[k, s, u] = remote.start(
                part.at[k, local_part(k, s, u, ring_owner(s, 0)), :],
                rs.at[k, s, u, 0], (rsa, rsb), (k, s, u, 0), z_way[s],
            )

    ring_start(0)
    for cp in weights[1]:
        cp.wait_recv()

    @pl.loop(0, 4)
    def _(i):
        dots(i, 1)

    ring_start(1)
    theirs = aligned((1 - h) * WIDTH, WIDTH)
    code_copies = [
        remote.start(
            codes.at[pl.ds(i * 128, 128), pl.ds(theirs, WIDTH)],
            codes_o.at[pl.ds(i * 128, 128), :],
            (ca, cb), i, partner,
        )
        for i in range(4)
    ]

    for step in range(1, 7):
        for k in range(2):
            for s, u in streams:
                ring[k, s, u].wait_recv()
                rs[k, s, u, step - 1] += part[k, local_part(k, s, u, ring_owner(s, step)), :]
                ring[k, s, u] = remote.start(
                    rs.at[k, s, u, step - 1], rs.at[k, s, u, step],
                    (rsa, rsb), (k, s, u, step), z_way[s],
                )

    for cp in code_parts:
        cp.wait()
    for cp in misc:
        cp.wait_recv()
    is_own = (z // 4) == h
    my_scales = jnp.where(
        is_own,
        sc[pl.ds(aligned(h * 16, 16), 16), pl.ds(row0, 128)].astype(f32),
        sc_other[:, pl.ds(row0, 128)].astype(f32),
    ).astype(bf16)
    squares = sq_mine[0:1, :] + sq_other[0:1, :]
    sq_o[...] = jnp.broadcast_to(squares, sq_o.shape)
    half_norms = (0.5 * penalty) * jnp.sqrt(squares + epsilon)
    sc_o[...] = sc_other[...]
    z_rows = aligned(z * 128, 128)

    def residual(k):
        wide_codes = jnp.where(is_own, mine_codes[k].astype(f32), other_codes[k].astype(f32))
        inputs = wide_codes * spread(my_scales, k * 8 + x * 2, PIECE)
        shift = bias[:, pl.ds(aligned(h * WIDTH + k * HALF + x * PIECE, PIECE), PIECE)]
        for s, u in streams:
            ring[k, s, u].wait_recv()
            recon = rs[k, s, u, 6] + part[k, local_part(k, s, u, z), :]
            first = s * 64 + u * 32
            value = (recon + shift - inputs[first : first + 32, :]).astype(bf16)
            resid[k, pl.ds(aligned(z * 128 + first, 32), 32), pl.ds(x_cols, PIECE)] = value

    def send_x(k, owner, sems, index):
        tile = resid.at[k, pl.ds(aligned(owner * 128, 128), 128), pl.ds(x_cols, PIECE)]
        return [
            remote.start(tile, tile, sems, (index, o - 1), at(xx=xp[o])) for o in (2, 1, 3)
        ]

    def block_at(way, distance):
        return (z + 8 - distance) % 8 if way == 0 else (z + distance) % 8

    zc = {}

    def send_z(k, way, j):
        sub = j % 2 if way == 0 else 1 - j % 2
        rows = pl.ds(aligned(block_at(way, j // 2) * 128 + sub * 64, 64), 64)
        cols = pl.ds(0, HALF) if k == 0 else pl.ds(x_cols, PIECE)
        tile = resid.at[k, rows, cols]
        sems = (z0a, z0b) if k == 0 else (z1a, z1b)
        zc[k, way, j] = remote.start(tile, tile, sems, (way, j), z_way[way])

    residual(0)
    x0 = send_x(0, z, (x0a, x0b), 0)
    residual(1)
    for way in range(2):
        for j in range(2):
            send_z(1, way, j)
    order = [z, block_at(0, 1), block_at(1, 1), block_at(0, 2), block_at(1, 2), block_at(0, 3), block_at(1, 3)]
    order.append((z + 4) % 8)
    x1 = [send_x(1, z, (x1a, x1b), 0)]
    for cp in x0:
        cp.wait_recv()
    for j in range(2):
        for way in range(2):
            send_z(0, way, j)
    for j in range(7):
        for way in range(2):
            zc[1, way, j].wait_recv()
            if j + 2 < 7:
                send_z(1, way, j + 2)
            if j % 2 == 1:
                x1.append(send_x(1, order[len(x1)], (x1a, x1b), len(x1)))
    x1.append(send_x(1, order[7], (x1a, x1b), 7))

    core_rows = aligned(c * 64, 64)
    y_rows = aligned(y * 16, 16)
    gc, gy, py, pc = {}, {}, {}, {}

    def first(i):
        for cp in x1[i]:
            cp.wait_recv()
        start = order[i] * 128
        rows = pl.ds(aligned(start, 128), 128)
        grad[i] = (
            lax.dot_general(resid[0, rows, :], w[:, :HALF], NT, preferred_element_type=f32)
            + lax.dot_general(resid[1, rows, :], w[:, HALF:], NT, preferred_element_type=f32)
            + half_norms
        )
        theirs = pl.ds(aligned((1 - c) * 64, 64), 64)
        gc[i] = remote.start(grad.at[i, theirs, :], core_in.at[i], (gca, gcb), i, sibling)

    def second(i):
        gc[i].wait_recv()
        core_sum[i] = core_in[i] + grad[i, pl.ds(core_rows, 64), :]
        gy[i] = [
            remote.start(
                core_sum.at[i, pl.ds(aligned(yp[o] * 16, 16), 16), :], y_in.at[i, o - 1],
                (gya, gyb), (i, o - 1), at(yy=yp[o]),
            )
            for o in (2, 1, 3)
        ]

    def third(i):
        for cp in gy[i]:
            cp.wait_recv()
        total = core_sum[i, pl.ds(y_rows, 16), :] + y_in[i, 0] + y_in[i, 1] + y_in[i, 2]
        rows = pl.ds(aligned(order[i] * 128 + c * 64 + y * 16, 16), 16)
        active = la[rows, pl.ds(my_cols, FB)].astype(f32) > 0
        pre[rows, :] = jnp.where(active, total, 0.0).astype(bf16)
        tile = pre.at[rows, :]
        py[i] = [remote.start(tile, tile, (pya, pyb), (i, o - 1), at(yy=yp[o])) for o in (2, 1, 3)]

    def fourth(i):
        for cp in py[i]:
            cp.wait_recv()
        tile = pre.at[pl.ds(aligned(order[i] * 128 + c * 64, 64), 64), :]
        pc[i] = remote.start(tile, tile, (pca, pcb), i, sibling)

    def stages(t):
        for lag, stage in enumerate((first, second, third, fourth)):
            if 0 <= t - lag < 8:
                stage(t - lag)

    stages(0)
    for j in range(7):
        for way in range(2):
            zc[0, way, j].wait_recv()
            if j + 2 < 7:
                send_z(0, way, j + 2)
            if j % 2 == 1:
                stages(j + way)
    out_copies = [
        pltpu.make_async_copy(resid, resid_o, local_sem.at[6]),
        pltpu.make_async_copy(la.at[:, pl.ds(my_cols, FB)], acts_o, local_sem.at[7]),
    ]
    stages(7)
    for cp in out_copies:
        cp.start()
    for t in range(8, 11):
        stages(t)
    for cp in pc.values():
        cp.wait_recv()
    pre_o[...] = pre[...]
    for cp in code_copies:
        cp.wait_recv()
    for cp in out_copies:
        cp.wait()
    remote.finish()


def exchange(lat, w, sc, bias, codes):
    vmem = pl.BlockSpec(memory_space=pltpu.VMEM)
    hbm = pl.BlockSpec(memory_space=pl.ANY)
    shape = jax.ShapeDtypeStruct
    pairs = [(3,), (2, 3), (3,), (4,), (2, 2, 2, 7), (1, 3), (2, 7), (2, 7), (8, 3), (8,), (8, 3), (8, 3), (8,), (4,), (4,)]
    return pl.pallas_call(
        exchange_kernel,
        out_shape=[
            shape((2, ROWS, HALF), bf16),
            shape((ROWS, FB), bf16),
            shape((ROWS, FB), bf16),
            shape((8, FB), f32),
            shape((ROWS // 2, WIDTH), bf16),
            shape((16, ROWS // 2), bf16),
        ],
        in_specs=[hbm, hbm, vmem, vmem, hbm],
        out_specs=[hbm, hbm, vmem, vmem, hbm, vmem],
        scratch_shapes=[
            pltpu.VMEM((ROWS, 4 * FB), bf16),
            pltpu.VMEM((FB, WIDTH), bf16),
            pltpu.VMEM((2, 4 * FB, PIECE), bf16),
            pltpu.VMEM((2, ROWS, PIECE), f32),
            pltpu.VMEM((2, 2, 2, 7, 32, PIECE), f32),
            pltpu.VMEM((2, ROWS, HALF), bf16),
            pltpu.VMEM((8, 128, FB), f32),
            pltpu.VMEM((8, 64, FB), f32),
            pltpu.VMEM((8, 64, FB), f32),
            pltpu.VMEM((8, 3, 16, FB), f32),
            pltpu.VMEM((ROWS, FB), bf16),
            pltpu.VMEM((2, 128, PIECE), bf16),
            pltpu.VMEM((2, 128, PIECE), bf16),
            pltpu.VMEM((8, FB), f32),
            pltpu.VMEM((8, FB), f32),
            pltpu.VMEM((16, ROWS // 2), bf16),
            pltpu.SemaphoreType.DMA((8,)),
        ]
        + [pltpu.SemaphoreType.DMA(count) for count in pairs for _ in range(2)],
        compiler_params=pltpu.CompilerParams(
            collective_id=0, has_side_effects=True, vmem_limit_bytes=50 * 2**20
        ),
        name="exchange",
    )(lat, w, sc, bias, codes)


def grads_kernel(half, acts, resid, w, pre, squares, own_codes, other_codes, own_sc, other_sc, enc_o, dec_o, bias_o):
    step = pl.program_id(0)
    h = half[0]
    act_sum = jnp.sum(acts[...].astype(f32), axis=0, keepdims=True)
    scale = penalty * act_sum / jnp.sqrt(squares[0:1, :] + epsilon)
    column = jnp.broadcast_to(scale, (128, 128)).T
    for k in range(2):
        term = lax.dot_general(acts[...], resid[k], TN, preferred_element_type=f32)
        for j in range(8):
            cols = slice(k * HALF + j * 128, k * HALF + j * 128 + 128)
            dec_o[pl.ds(k * 8 + j, 128, stride=16), :] = (
                term[:, j * 128 : j * 128 + 128] + column * w[:, cols].astype(f32)
            )
    own_at = pl.multiple_of(h * 512, 512)
    other_at = pl.multiple_of((1 - h) * 512, 512)
    own_in = (own_codes[...].astype(f32) * spread(own_sc[...], step * 4, 512)).astype(bf16)
    other_in = (other_codes[...].astype(f32) * spread(other_sc[...], step * 4, 512)).astype(bf16)
    enc = lax.dot_general(own_in, pre[pl.ds(own_at, 512), :], TN, preferred_element_type=f32)
    enc += lax.dot_general(other_in, pre[pl.ds(other_at, 512), :], TN, preferred_element_type=f32)
    for j in range(4):
        enc_o[pl.ds(j, 512, stride=4), :] = enc[:, j * 128 : j * 128 + 128]

    @pl.when(step == 0)
    def _():
        bias_o[...] = jnp.broadcast_to(jnp.sum(pre[...].astype(f32), axis=0, keepdims=True), bias_o.shape)


def grads(half, acts, resid, w, pre, squares, codes, other_codes, sc, other_sc):
    whole = lambda *shape: pl.BlockSpec(shape, lambda i, h: (0,) * len(shape))
    return pl.pallas_call(
        grads_kernel,
        grid_spec=pltpu.PrefetchScalarGridSpec(
            num_scalar_prefetch=1,
            grid=(4,),
            in_specs=[
                pl.BlockSpec((ROWS, 128), lambda i, h: (0, i)),
                whole(2, ROWS, HALF),
                pl.BlockSpec((128, WIDTH), lambda i, h: (i, 0)),
                whole(ROWS, FB),
                pl.BlockSpec((8, 128), lambda i, h: (0, i)),
                pl.BlockSpec((512, 512), lambda i, h: (0, h[0] * 4 + i)),
                pl.BlockSpec((512, 512), lambda i, h: (0, i)),
                pl.BlockSpec((16, 512), lambda i, h: (h[0], 0)),
                whole(16, 512),
            ],
            out_specs=[
                pl.BlockSpec((2048, 128), lambda i, h: (i, 0)),
                pl.BlockSpec((2048, 128), lambda i, h: (i, 0)),
                whole(8, FB),
            ],
        ),
        out_shape=[
            jax.ShapeDtypeStruct((WIDTH * 4, 128), f32),
            jax.ShapeDtypeStruct((FB * 16, 128), f32),
            jax.ShapeDtypeStruct((8, FB), f32),
        ],
        compiler_params=pltpu.CompilerParams(vmem_limit_bytes=50 * 2**20),
        name="grads",
    )(half, acts, resid, w, pre, squares, codes, other_codes, sc, other_sc)


def shards(act_codes, act_scales, latents, dec_weight, dec_bias):
    w = dec_weight[:, 0, :]
    codes = act_codes[:, 0, :]
    sc = act_scales[:, 0, :].T
    resid, acts, pre, squares, other_codes, other_sc = exchange(latents, w, sc, dec_bias, codes)
    half = lax.axis_index("dp").astype(jnp.int32).reshape(1)
    enc, dec, bias = grads(half, acts, resid, w, pre, squares, codes, other_codes, sc, other_sc)
    return enc.reshape(WIDTH, 1, FB), dec.reshape(FB, 1, WIDTH), bias[0]


def solution(mesh):
    in_specs = (
        P("dp", "lyr", None),
        P("dp", "lyr", None),
        P("dp", "lat"),
        P("lat", "lyr", "dp"),
        P("lyr", None),
    )
    out_specs = (P("dp", "lyr", "lat"), P("lat", "lyr", "dp"), P("lat"))
    return jax.shard_map(shards, mesh=mesh, in_specs=in_specs, out_specs=out_specs, check_vma=False)
```

time: 596 us -> 143 us (0.24)
  waiting for transfers between devices: 470 us -> 0 us
  Pallas kernels: 0 us -> 139 us
  local copies, waits for them, and re-layouts: 40.7 us -> 3.09 us
  matrix products: 32.8 us -> 0 us
  other arithmetic: 18.6 us -> 0 us
  blocking collectives: 18.2 us -> 0 us
  between operations: 13.8 us -> 0.65 us
    psum x2 -> x0, waiting for transfers between devices: 217 us -> none  [the longest x1 195 us: reconstruct(): recon = lax.psum(partial_value, 'lat')]
    reduce_scatter x2 -> x0, waiting for transfers between devices: 183 us -> none  [the longest x1 91.9 us: shards(): lax.psum_scatter(jnp.einsum('rld,rf->dlf', inputs_bf, grad_pre, preferred...]
    pallas_call x0 -> x2, Pallas kernels: none -> 139 us  [the longest x1 127 us: exchange(): pl.pallas_call(exchange_kernel, out_shape=[shape((2, ROWS, HALF), bf16),...]
    all_gather x1 -> x0, waiting for transfers between devices: 69.1 us -> none  [shards(): weight = lax.all_gather(dec_weight, 'dp', axis=2, tiled=True)]
    dot_general x4 -> x0, matrix products: 32.8 us -> none  [the longest x1 10.2 us: shards(): jnp.einsum('rld,rf->dlf', inputs_bf, grad_pre, preferred_element_type=jnp...]
    unnamed x9 -> x6, local copies, waits for them, and re-layouts: 25.5 us -> 2.51 us
    psum x3 -> x0, blocking collectives: 18.2 us -> none  [the longest x2 11.2 us: shards(): lax.psum((local_squares, jnp.sum(latents.astype(jnp.float32), axis=0)), '...]
    mul x3 -> x0, local copies, waits for them, and re-layouts: 15.3 us -> none  [dequantize(): code_block.astype(jnp.float32)]
  transfers between devices with their start and end apart: 5 -> 0, of which waited for: 5 -> 0; matrix products, arithmetic and copies ran while one was open for 9% -> 0% of each run, Pallas kernels for 0% -> 0%
where the time goes in v3:
time: 143 us
  Pallas kernels  139 us (97%)
  local copies, waits for them, and re-layouts  3.09 us (2%)
    pallas_call x1, Pallas kernels, exchange(): pl.pallas_call(exchange_kernel, out_shape=[shape((2, ROWS, HALF), bf16),...  127 us
    pallas_call x1, Pallas kernels, grads(): pl.pallas_call(grads_kernel, grid_spec=pltpu.PrefetchScalarGridSpec(num_s...  12.4 us

profile of v3, /device:TPU:1, one launch (start us, length us, event | category | flops | bytes accessed | tf_op | source)
XLA Modules:
  0.0 143.1 jit_solution(9971508439210505908)
XLA Ops:
  0.6 0.0 copy-start
  0.6 1.0 copy-done
  1.7 0.0 copy-start.1
  1.7 0.8 copy-done.1
  2.4 0.0 copy-start.2
  2.4 0.7 copy-done.2
  3.2 127.0 %exchange.1 = (bf16[2,1024,1024]{2,1,0:T(8,128)(2,1)}, bf16[1024,512]{1,0:T(8,128)(2,1)S(1)}, bf16[1024,512]{1,0:T(8,128)(2,1)S(1)}, f32[8,512]{1,0:T(8,128)S(1)...) custom-call(bf16[512,512]{1,0:T(8,128)(2,1)S(1)} %copy-done, bf16[512,2048]{1,0:T(8,128)(2,1)} %bitcast.13, ...), custom_call_target="tpu_custom_call" | custom-call | tf_op jit(solution)/shard_map/exchange/pallas_call | solution.py:393
  130.2 12.4 %grads.1 = (f32[8192,128]{1,0:T(8,128)}, f32[8192,128]{1,0:T(8,128)}, f32[8,512]{1,0:T(8,128)S(1)}) custom-call(s32[1]{0:T(128)} %bitcast.half, bf16[1024,512]{1,0:T(8,128)(2,1)S(1)} %get-tuple-element.12.acts, bf16[2,1024,1024]{2,1,0:T(8,128)(2,1)} %get-tuple-element.13.resid, bf16[512,2048]{1,0:T(8,128)(2,1)} %bitcast.14, ...), custom_call_target="tpu_custom_call" | custom-call | tf_op jit(solution)/shard_map/grads/pallas_call | solution.py:461
  142.5 0.6 slice.3
Async XLA Ops:
  0.6 1.0 copy-start
  1.7 0.8 copy-start.1
  2.4 0.7 copy-start.2

commit v4 on v3

--- a/solution.py
+++ b/solution.py
@@ -15,6 +15,8 @@
 ROWS, FB, WIDTH = 1024, 512, 2048
 HALF = WIDTH // 2
 PIECE = HALF // 4
+LAG = 0
+VMEM_LIMIT = 56 * 2**20
 NT = (((1,), (1,)), ((), ()))
 TN = (((0,), (0,)), ((), ()))
 
@@ -55,8 +57,8 @@
 
 def exchange_kernel(
     lat, w_hbm, sc, bias, codes,
-    resid_o, acts_o, pre_o, sq_o, codes_o, sc_o,
-    la, w, wx, part, rs, resid, grad, core_in, core_sum, y_in, pre, mine_codes, other_codes, sq_mine, sq_other, sc_other,
+    resid_o, acts_o, pre_o, sq_o, in_o,
+    la, w, wx, part, rs, resid, grad, core_in, core_sum, y_in, pre, mine_codes, other_codes, sq_mine, sq_other, sc_other, codes_v, sc_wide, turned, w_t,
     local_sem,
     l1a, l1b, wa, wb, l2a, l2b, l3a, l3b, rsa, rsb, x0a, x0b, z0a, z0b, z1a, z1b, x1a, x1b,
     gca, gcb, gya, gyb, pya, pyb, pca, pcb, ma, mb, ca, cb,
@@ -99,6 +101,7 @@
                 local_sem.at[2 + k],
             )
         )
+    codes_copy = pltpu.make_async_copy(codes, codes_v, local_sem.at[8])
     code_parts = []
     for k in range(2):
         ours = aligned(h * WIDTH + k * HALF + x * PIECE, PIECE)
@@ -107,7 +110,7 @@
                 codes.at[pl.ds(row0, 128), pl.ds(ours, PIECE)], mine_codes.at[k], local_sem.at[4 + k]
             )
         )
-    for cp in own_copies + code_parts:
+    for cp in own_copies + code_parts + [codes_copy]:
         cp.start()
 
     barrier = pltpu.get_barrier_semaphore()
@@ -124,17 +127,6 @@
             (l1a, l1b), o - 1, at(xx=xp[o]),
         )
         for o in (1, 2, 3)
-    ]
-    weights = [
-        [
-            remote.start(
-                w_hbm.at[:, pl.ds(aligned(k * HALF + xp[o] * PIECE, PIECE), PIECE)],
-                wx.at[k, pl.ds(my_cols, FB), :],
-                (wa, wb), (k, o - 1), at(xx=xp[o]),
-            )
-            for o in (1, 2, 3)
-        ]
-        for k in range(2)
     ]
     misc = []
     for k in range(2):
@@ -151,7 +143,18 @@
     for cp in l1:
         cp.wait_recv()
     block = la.at[pl.ds(my_block, 128), :]
-    l2 = {o: remote.start(block, block, (l2a, l2b), o - 1, at(yy=yp[o])) for o in (2, 1, 3)}
+    l2 = {o: remote.start(block, block, (l2a, l2b), o - 1, at(yy=yp[o])) for o in (1, 3)}
+    weights = [
+        [
+            remote.start(
+                w_hbm.at[:, pl.ds(aligned(k * HALF + xp[o] * PIECE, PIECE), PIECE)],
+                wx.at[k, pl.ds(my_cols, FB), :],
+                (wa, wb), (k, o - 1), at(xx=xp[o]),
+            )
+            for o in (1, 2, 3)
+        ]
+        for k in range(2)
+    ]
     l3 = [remote.start(block, block, (l3a, l3b), 0, sibling)]
 
     w_copy.wait()
@@ -170,30 +173,52 @@
 
     misc.append(remote.start(sq_mine, sq_other, (ma, mb), 3, partner))
 
+    def turn_weights(i, carry):
+        cols = pl.ds(aligned(i * 128, 128), 128)
+        w_t[cols, :] = w[:, cols].astype(f32).T.astype(bf16)
+        return carry
+
+    lax.fori_loop(0, 16, turn_weights, 0)
+
     def dots(chunk, k):
         rows = aligned(chunk * 256, 256)
         part[k, pl.ds(rows, 256), :] = jnp.dot(
             la[pl.ds(rows, 256), :], wx[k], preferred_element_type=f32
         )
 
-    def pass_on(o, index):
+    codes_copy.wait()
+    sc_wide[...] = sc[...].astype(f32)
+
+    def turn(i, carry):
+        cols = pl.ds(aligned(i * 128, 128), 128)
+        turned[cols, :] = (codes_v[:, cols].astype(f32).T * sc_wide[pl.ds(i, 1), :]).astype(bf16)
+        return carry
+
+    lax.fori_loop(0, 16, turn, 0)
+
+    def rows_of(yy, cc, part_of=0, parts=1):
+        count = 128 // parts
+        return la.at[pl.ds(aligned((yy * 2 + cc) * 128 + part_of * count, count), count), :]
+
+    for o in (1, 3):
         l2[o].wait_recv()
-        arrived = la.at[pl.ds(aligned((yp[4 - o] * 2 + c) * 128, 128), 128), :]
-        l3.append(remote.start(arrived, arrived, (l3a, l3b), index, sibling))
-
-    for cp in weights[0]:
-        cp.wait_recv()
-    l3[0].wait_recv()
-    dots(y, 0)
-    pass_on(3, 1)
-    pass_on(1, 2)
-    l3[1].wait_recv()
-    dots(yp[1], 0)
-    pass_on(2, 3)
-    l3[2].wait_recv()
-    dots(yp[3], 0)
-    l3[3].wait_recv()
-    dots(yp[2], 0)
+        arrived = rows_of(yp[4 - o], c)
+        l3.append(remote.start(arrived, arrived, (l3a, l3b), o, sibling))
+        half = rows_of(yp[4 - o], c, 0 if o == 1 else 1, 2)
+        l2[o, 2] = remote.start(half, half, (l2a, l2b), 1 if o == 1 else 3, at(yy=yp[o]))
+
+    lax.fori_loop(16, 32, turn, 0)
+    for o in (1, 3):
+        l2[o, 2].wait_recv()
+    arrived = rows_of(yp[2], c)
+    l3.append(remote.start(arrived, arrived, (l3a, l3b), 2, sibling))
+
+    for cp in weights[0] + l3:
+        cp.wait_recv()
+
+    @pl.loop(0, 4)
+    def _(i):
+        dots(i, 0)
 
     def local_part(k, s, u, owner):
         return pl.ds(aligned(owner * 128 + s * 64 + u * 32, 32), 32)
@@ -220,16 +245,22 @@
         dots(i, 1)
 
     ring_start(1)
-    theirs = aligned((1 - h) * WIDTH, WIDTH)
-    code_copies = [
+    in_copies = [
+        pltpu.make_async_copy(
+            turned.at[pl.ds(aligned(h * WIDTH, WIDTH), WIDTH), :],
+            in_o.at[h],
+            local_sem.at[9],
+        )
+    ]
+    in_copies[0].start()
+    in_sends = [
         remote.start(
-            codes.at[pl.ds(i * 128, 128), pl.ds(theirs, WIDTH)],
-            codes_o.at[pl.ds(i * 128, 128), :],
+            turned.at[pl.ds(aligned((1 - h) * WIDTH + i * 512, 512), 512), :],
+            in_o.at[h, pl.ds(i * 512, 512), :],
             (ca, cb), i, partner,
         )
         for i in range(4)
     ]
-
     for step in range(1, 7):
         for k in range(2):
             for s, u in streams:
@@ -253,7 +284,6 @@
     squares = sq_mine[0:1, :] + sq_other[0:1, :]
     sq_o[...] = jnp.broadcast_to(squares, sq_o.shape)
     half_norms = (0.5 * penalty) * jnp.sqrt(squares + epsilon)
-    sc_o[...] = sc_other[...]
     z_rows = aligned(z * 128, 128)
 
     def residual(k):
@@ -319,8 +349,8 @@
         start = order[i] * 128
         rows = pl.ds(aligned(start, 128), 128)
         grad[i] = (
-            lax.dot_general(resid[0, rows, :], w[:, :HALF], NT, preferred_element_type=f32)
-            + lax.dot_general(resid[1, rows, :], w[:, HALF:], NT, preferred_element_type=f32)
+            jnp.dot(resid[0, rows, :], w_t[:HALF, :], preferred_element_type=f32)
+            + jnp.dot(resid[1, rows, :], w_t[HALF:, :], preferred_element_type=f32)
             + half_norms
         )
         theirs = pl.ds(aligned((1 - c) * 64, 64), 64)
@@ -358,29 +388,28 @@
             if 0 <= t - lag < 8:
                 stage(t - lag)
 
-    stages(0)
     for j in range(7):
         for way in range(2):
             zc[0, way, j].wait_recv()
             if j + 2 < 7:
                 send_z(0, way, j + 2)
-            if j % 2 == 1:
-                stages(j + way)
+        if j >= LAG:
+            stages(j - LAG)
     out_copies = [
         pltpu.make_async_copy(resid, resid_o, local_sem.at[6]),
         pltpu.make_async_copy(la.at[:, pl.ds(my_cols, FB)], acts_o, local_sem.at[7]),
     ]
-    stages(7)
-    for cp in out_copies:
-        cp.start()
-    for t in range(8, 11):
+    for t in range(7 - LAG, 11):
         stages(t)
+        if t == 7:
+            for cp in out_copies:
+                cp.start()
     for cp in pc.values():
         cp.wait_recv()
     pre_o[...] = pre[...]
-    for cp in code_copies:
-        cp.wait_recv()
-    for cp in out_copies:
+    for cp in in_sends:
+        cp.wait_recv()
+    for cp in out_copies + in_copies:
         cp.wait()
     remote.finish()
 
@@ -389,7 +418,7 @@
     vmem = pl.BlockSpec(memory_space=pltpu.VMEM)
     hbm = pl.BlockSpec(memory_space=pl.ANY)
     shape = jax.ShapeDtypeStruct
-    pairs = [(3,), (2, 3), (3,), (4,), (2, 2, 2, 7), (1, 3), (2, 7), (2, 7), (8, 3), (8,), (8, 3), (8, 3), (8,), (4,), (4,)]
+    pairs = [(3,), (2, 3), (4,), (4,), (2, 2, 2, 7), (1, 3), (2, 7), (2, 7), (8, 3), (8,), (8, 3), (8, 3), (8,), (4,), (4,)]
     return pl.pallas_call(
         exchange_kernel,
         out_shape=[
@@ -397,11 +426,10 @@
             shape((ROWS, FB), bf16),
             shape((ROWS, FB), bf16),
             shape((8, FB), f32),
-            shape((ROWS // 2, WIDTH), bf16),
-            shape((16, ROWS // 2), bf16),
+            shape((2, WIDTH, ROWS // 2), bf16),
         ],
         in_specs=[hbm, hbm, vmem, vmem, hbm],
-        out_specs=[hbm, hbm, vmem, vmem, hbm, vmem],
+        out_specs=[hbm, hbm, vmem, vmem, hbm],
         scratch_shapes=[
             pltpu.VMEM((ROWS, 4 * FB), bf16),
             pltpu.VMEM((FB, WIDTH), bf16),
@@ -419,19 +447,21 @@
             pltpu.VMEM((8, FB), f32),
             pltpu.VMEM((8, FB), f32),
             pltpu.VMEM((16, ROWS // 2), bf16),
-            pltpu.SemaphoreType.DMA((8,)),
+            pltpu.VMEM((ROWS // 2, 2 * WIDTH), bf16),
+            pltpu.VMEM((32, ROWS // 2), f32),
+            pltpu.VMEM((2 * WIDTH, ROWS // 2), bf16),
+            pltpu.VMEM((WIDTH, FB), bf16),
+            pltpu.SemaphoreType.DMA((10,)),
         ]
         + [pltpu.SemaphoreType.DMA(count) for count in pairs for _ in range(2)],
         compiler_params=pltpu.CompilerParams(
-            collective_id=0, has_side_effects=True, vmem_limit_bytes=50 * 2**20
+            collective_id=0, has_side_effects=True, vmem_limit_bytes=VMEM_LIMIT
         ),
         name="exchange",
     )(lat, w, sc, bias, codes)
 
 
-def grads_kernel(half, acts, resid, w, pre, squares, own_codes, other_codes, own_sc, other_sc, enc_o, dec_o, bias_o):
-    step = pl.program_id(0)
-    h = half[0]
+def grads_kernel(acts, resid, w, pre, squares, inputs, enc_o, dec_o, bias_o):
     act_sum = jnp.sum(acts[...].astype(f32), axis=0, keepdims=True)
     scale = penalty * act_sum / jnp.sqrt(squares[0:1, :] + epsilon)
     column = jnp.broadcast_to(scale, (128, 128)).T
@@ -442,62 +472,51 @@
             dec_o[pl.ds(k * 8 + j, 128, stride=16), :] = (
                 term[:, j * 128 : j * 128 + 128] + column * w[:, cols].astype(f32)
             )
-    own_at = pl.multiple_of(h * 512, 512)
-    other_at = pl.multiple_of((1 - h) * 512, 512)
-    own_in = (own_codes[...].astype(f32) * spread(own_sc[...], step * 4, 512)).astype(bf16)
-    other_in = (other_codes[...].astype(f32) * spread(other_sc[...], step * 4, 512)).astype(bf16)
-    enc = lax.dot_general(own_in, pre[pl.ds(own_at, 512), :], TN, preferred_element_type=f32)
-    enc += lax.dot_general(other_in, pre[pl.ds(other_at, 512), :], TN, preferred_element_type=f32)
+    enc = jnp.dot(inputs[0], pre[: ROWS // 2, :], preferred_element_type=f32)
+    enc += jnp.dot(inputs[1], pre[ROWS // 2 :, :], preferred_element_type=f32)
     for j in range(4):
         enc_o[pl.ds(j, 512, stride=4), :] = enc[:, j * 128 : j * 128 + 128]
 
-    @pl.when(step == 0)
+    @pl.when(pl.program_id(0) == 0)
     def _():
-        bias_o[...] = jnp.broadcast_to(jnp.sum(pre[...].astype(f32), axis=0, keepdims=True), bias_o.shape)
-
-
-def grads(half, acts, resid, w, pre, squares, codes, other_codes, sc, other_sc):
-    whole = lambda *shape: pl.BlockSpec(shape, lambda i, h: (0,) * len(shape))
+        bias_o[...] = jnp.sum(pre[...].astype(f32), axis=0, keepdims=True)
+
+
+def grads(acts, resid, w, pre, squares, inputs):
+    whole = lambda *shape: pl.BlockSpec(shape, lambda i: (0,) * len(shape))
     return pl.pallas_call(
         grads_kernel,
-        grid_spec=pltpu.PrefetchScalarGridSpec(
-            num_scalar_prefetch=1,
-            grid=(4,),
-            in_specs=[
-                pl.BlockSpec((ROWS, 128), lambda i, h: (0, i)),
-                whole(2, ROWS, HALF),
-                pl.BlockSpec((128, WIDTH), lambda i, h: (i, 0)),
-                whole(ROWS, FB),
-                pl.BlockSpec((8, 128), lambda i, h: (0, i)),
-                pl.BlockSpec((512, 512), lambda i, h: (0, h[0] * 4 + i)),
-                pl.BlockSpec((512, 512), lambda i, h: (0, i)),
-                pl.BlockSpec((16, 512), lambda i, h: (h[0], 0)),
-                whole(16, 512),
-            ],
-            out_specs=[
-                pl.BlockSpec((2048, 128), lambda i, h: (i, 0)),
-                pl.BlockSpec((2048, 128), lambda i, h: (i, 0)),
-                whole(8, FB),
-            ],
-        ),
+        grid=(4,),
+        in_specs=[
+            pl.BlockSpec((ROWS, 128), lambda i: (0, i)),
+            whole(2, ROWS, HALF),
+            pl.BlockSpec((128, WIDTH), lambda i: (i, 0)),
+            whole(ROWS, FB),
+            pl.BlockSpec((8, 128), lambda i: (0, i)),
+            pl.BlockSpec((2, 512, ROWS // 2), lambda i: (0, i, 0)),
+        ],
+        out_specs=[
+            pl.BlockSpec((2048, 128), lambda i: (i, 0)),
+            pl.BlockSpec((2048, 128), lambda i: (i, 0)),
+            whole(1, FB),
+        ],
         out_shape=[
             jax.ShapeDtypeStruct((WIDTH * 4, 128), f32),
             jax.ShapeDtypeStruct((FB * 16, 128), f32),
-            jax.ShapeDtypeStruct((8, FB), f32),
+            jax.ShapeDtypeStruct((1, FB), f32),
         ],
         compiler_params=pltpu.CompilerParams(vmem_limit_bytes=50 * 2**20),
         name="grads",
-    )(half, acts, resid, w, pre, squares, codes, other_codes, sc, other_sc)
+    )(acts, resid, w, pre, squares, inputs)
 
 
 def shards(act_codes, act_scales, latents, dec_weight, dec_bias):
     w = dec_weight[:, 0, :]
-    codes = act_codes[:, 0, :]
-    sc = act_scales[:, 0, :].T
-    resid, acts, pre, squares, other_codes, other_sc = exchange(latents, w, sc, dec_bias, codes)
-    half = lax.axis_index("dp").astype(jnp.int32).reshape(1)
-    enc, dec, bias = grads(half, acts, resid, w, pre, squares, codes, other_codes, sc, other_sc)
-    return enc.reshape(WIDTH, 1, FB), dec.reshape(FB, 1, WIDTH), bias[0]
+    resid, acts, pre, squares, inputs = exchange(
+        latents, w, act_scales[:, 0, :].T, dec_bias, act_codes[:, 0, :]
+    )
+    enc, dec, bias = grads(acts, resid, w, pre, squares, inputs)
+    return enc.reshape(WIDTH, 1, FB), dec.reshape(FB, 1, WIDTH), bias.reshape(FB)
 
 
 def solution(mesh):

time: 143 us -> 137 us (0.958)
  Pallas kernels: 139 us -> 133 us
    pallas_call x1, Pallas kernels: 127 us -> 122 us  [exchange(): pl.pallas_call(exchange_kernel, out_shape=[shape((2, ROWS, HALF), bf16),...]
where the time goes in v4:
time: 137 us
  Pallas kernels  133 us (97%)
  local copies, waits for them, and re-layouts  3.16 us (2%)
    pallas_call x1, Pallas kernels, exchange(): pl.pallas_call(exchange_kernel, out_shape=[shape((2, ROWS, HALF), bf16),...  122 us
    pallas_call x1, Pallas kernels, grads(): pl.pallas_call(grads_kernel, grid=(4,), in_specs=[pl.BlockSpec((ROWS, 128...  11 us
    unnamed x6, local copies, waits for them, and re-layouts  3.16 us

profile of v4, /device:TPU:1, one launch (start us, length us, event | category | flops | bytes accessed | tf_op | source)
XLA Modules:
  0.0 136.9 jit_solution(1018469016081006931)
XLA Ops:
  0.6 122.1 %exchange.1 = (bf16[2,1024,1024]{2,1,0:T(8,128)(2,1)}, bf16[1024,512]{1,0:T(8,128)(2,1)}, bf16[1024,512]{1,0:T(8,128)(2,1)}, f32[8,512]{1,0:T(8,128)}, bf16[2,2048,512]{2,1,0:T(8,128)(2,1)}) custom-call(bf16[512,512]{1,0:T(8,128)(2,1)} %lat.1, bf16[512,2048]{1,0:T(8,128)(2,1)} %bitcast.8, bf16[32,512]{1,0:T(8,128)(2,1)} %bitcast.11, f32[1,4096]{1,0:T(1,128)} %bias.1, ...), custom_call_target="tpu_custom_call" | custom-call | tf_op jit(solution)/shard_map/exchange/pallas_call | solution.py:422
  122.8 0.0 copy-start
  122.8 1.2 copy-done
  124.0 0.0 copy-start.1
  124.0 1.2 copy-done.1
  125.2 0.0 copy-start.2
  125.2 0.7 copy-done.2
  125.9 11.0 %grads.1 = (f32[8192,128]{1,0:T(8,128)}, f32[8192,128]{1,0:T(8,128)}, f32[1,512]{1,0:T(1,128)}) custom-call(bf16[1024,512]{1,0:T(8,128)(2,1)S(1)} %copy-done, bf16[2,1024,1024]{2,1,0:T(8,128)(2,1)} %get-tuple-element.12.resid, bf16[512,2048]{1,0:T(8,128)(2,1)} %bitcast.9, bf16[1024,512]{1,0:T(8,128)(2,1)S(1)} %copy-done.1, f32[8,512]{1,0:T(8,128)S(1)} %copy-done.2, ...), custom_call_target="tpu_custom_call" | custom-call | tf_op jit(solution)/shard_map/grads/pallas_call | solution.py:487
Async XLA Ops:
  122.8 1.2 copy-start
  124.0 1.2 copy-start.1
  125.2 0.7 copy-start.2

commit v5 on v4

--- a/solution.py
+++ b/solution.py
@@ -15,7 +15,7 @@
 ROWS, FB, WIDTH = 1024, 512, 2048
 HALF = WIDTH // 2
 PIECE = HALF // 4
-LAG = 0
+LAGS = (0, 1, 3, 5)
 VMEM_LIMIT = 56 * 2**20
 NT = (((1,), (1,)), ((), ()))
 TN = (((0,), (0,)), ((), ()))
@@ -384,7 +384,7 @@
         pc[i] = remote.start(tile, tile, (pca, pcb), i, sibling)
 
     def stages(t):
-        for lag, stage in enumerate((first, second, third, fourth)):
+        for lag, stage in zip(LAGS, (first, second, third, fourth)):
             if 0 <= t - lag < 8:
                 stage(t - lag)
 
@@ -393,13 +393,12 @@
             zc[0, way, j].wait_recv()
             if j + 2 < 7:
                 send_z(0, way, j + 2)
-        if j >= LAG:
-            stages(j - LAG)
+        stages(j)
     out_copies = [
         pltpu.make_async_copy(resid, resid_o, local_sem.at[6]),
         pltpu.make_async_copy(la.at[:, pl.ds(my_cols, FB)], acts_o, local_sem.at[7]),
     ]
-    for t in range(7 - LAG, 11):
+    for t in range(7, 8 + LAGS[-1]):
         stages(t)
         if t == 7:
             for cp in out_copies:
@@ -416,7 +415,7 @@
 
 def exchange(lat, w, sc, bias, codes):
     vmem = pl.BlockSpec(memory_space=pltpu.VMEM)
-    hbm = pl.BlockSpec(memory_space=pl.ANY)
+    hbm = pl.BlockSpec(memory_space=pltpu.HBM)
     shape = jax.ShapeDtypeStruct
     pairs = [(3,), (2, 3), (4,), (4,), (2, 2, 2, 7), (1, 3), (2, 7), (2, 7), (8, 3), (8,), (8, 3), (8, 3), (8,), (4,), (4,)]
     return pl.pallas_call(

time: 137 us -> 135 us (0.985)
  Pallas kernels: 133 us -> 131 us
    pallas_call x1, Pallas kernels: 122 us -> 120 us  [exchange(): pl.pallas_call(exchange_kernel, out_shape=[shape((2, ROWS, HALF), bf16),...]
where the time goes in v5:
time: 135 us
  Pallas kernels  131 us (97%)
  local copies, waits for them, and re-layouts  3.16 us (2%)
    pallas_call x1, Pallas kernels, exchange(): pl.pallas_call(exchange_kernel, out_shape=[shape((2, ROWS, HALF), bf16),...  120 us
    pallas_call x1, Pallas kernels, grads(): pl.pallas_call(grads_kernel, grid=(4,), in_specs=[pl.BlockSpec((ROWS, 128...  11 us
    unnamed x6, local copies, waits for them, and re-layouts  3.16 us

profile of v5, /device:TPU:1, one launch (start us, length us, event | category | flops | bytes accessed | tf_op | source)
XLA Modules:
  0.0 134.7 jit_solution(11201371892129763432)
XLA Ops:
  0.6 119.9 %exchange.1 = (bf16[2,1024,1024]{2,1,0:T(8,128)(2,1)}, bf16[1024,512]{1,0:T(8,128)(2,1)}, bf16[1024,512]{1,0:T(8,128)(2,1)}, f32[8,512]{1,0:T(8,128)}, bf16[2,2048,512]{2,1,0:T(8,128)(2,1)}) custom-call(bf16[512,512]{1,0:T(8,128)(2,1)} %lat.1, bf16[512,2048]{1,0:T(8,128)(2,1)} %bitcast.8, bf16[32,512]{1,0:T(8,128)(2,1)} %bitcast.11, f32[1,4096]{1,0:T(1,128)} %bias.1, ...), custom_call_target="tpu_custom_call" | custom-call | tf_op jit(solution)/shard_map/exchange/pallas_call | solution.py:421
  120.6 0.0 copy-start
  120.6 1.2 copy-done
  121.8 0.0 copy-start.1
  121.8 1.2 copy-done.1
  123.0 0.0 copy-start.2
  123.0 0.7 copy-done.2
  123.7 11.0 %grads.1 = (f32[8192,128]{1,0:T(8,128)}, f32[8192,128]{1,0:T(8,128)}, f32[1,512]{1,0:T(1,128)}) custom-call(bf16[1024,512]{1,0:T(8,128)(2,1)S(1)} %copy-done, bf16[2,1024,1024]{2,1,0:T(8,128)(2,1)} %get-tuple-element.12.resid, bf16[512,2048]{1,0:T(8,128)(2,1)} %bitcast.9, bf16[1024,512]{1,0:T(8,128)(2,1)S(1)} %copy-done.1, f32[8,512]{1,0:T(8,128)S(1)} %copy-done.2, ...), custom_call_target="tpu_custom_call" | custom-call | tf_op jit(solution)/shard_map/grads/pallas_call | solution.py:486
Async XLA Ops:
  120.6 1.2 copy-start
  121.8 1.2 copy-start.1
  123.0 0.7 copy-start.2
